TPU v7x, 128 devices: a whole 4x4x4 slice. The times are simulated.
128 devices in a mesh: pipe: 8 (over x, y_hi), expert: 2 (over core), dp: 8 (over y_lo, z).
Axes of the slice: x: 4, y: 4 (y_hi: 2, y_lo: 2; y = y_hi * 2 + y_lo), z: 4, core: 2. Of those that a mesh axis runs over, the one named last changes fastest.
Arguments:
- hidden_in: bfloat16 [16384, 6144], P(('pipe', 'expert', 'dp'))
- norm_gain: float32 [8, 6144], P('pipe'), may hold values from 0.1 to 1.9
- w_gate: bfloat16 [8, 6144, 8192], P('pipe', None, ('expert', 'dp')), may hold values from -0.078125 to 0.078125
- w_up: bfloat16 [8, 6144, 8192], P('pipe', None, ('expert', 'dp')), may hold values from -0.078125 to 0.078125
- w_down: bfloat16 [8, 8192, 6144], P('pipe', ('expert', 'dp')), may hold values from -0.0625 to 0.0625
- expert_ids: int32 [16384, 2], P(('pipe', 'expert', 'dp')), may hold values from 0 to 7, as said below
- gate_weights: float32 [16384, 2], P(('pipe', 'expert', 'dp')), may hold values from 0.25 to 1
Outputs:
- passed_on: bfloat16 [16384, 6144], P(('pipe', 'expert', 'dp'))
Inputs may be any that keep to these rules, and one draw needn't show every extreme that they name: `expert_ids`: the two ids of a row differ. In every aligned block of 128 rows (the rows of one device) at most 64 rows name expert 0, and in each section's 16 blocks at least one block has 64 such rows; the 16 blocks of one section hold exactly 512 rows that name expert 0.
All inputs are finite; a program needn't handle non-finite values.
Results may differ from a plain program's by a relative error of at most 0.0045.
Values may be sent and summed in bfloat16 or wider, within the bound.
A program may use at most 192 MiB of HBM per device.

v0:
```python
import jax
import jax.numpy as jnp
from jax import lax
from jax.sharding import PartitionSpec as P


def passed_along(block, axis, distance):
    devices = range(lax.axis_size(axis))
    route = [((i - distance) % len(devices), i) for i in devices]
    return lax.ppermute(block, axis, route)


def rms_scale(values_in, gain):
    values = values_in.astype(jnp.float32)
    mean_sq = jnp.mean(values * values, axis=-1, keepdims=True)
    return (values * lax.rsqrt(mean_sq + 1e-05) * gain).astype(jnp.bfloat16)


def expert_rows(normed, gate_matrix, up_matrix, down_matrix):
    gate = jnp.dot(normed, gate_matrix, preferred_element_type=jnp.float32)
    up_values = jnp.dot(normed, up_matrix, preferred_element_type=jnp.float32)
    hidden = (jax.nn.silu(gate) * up_values).astype(jnp.bfloat16)
    return jnp.dot(hidden, down_matrix, preferred_element_type=jnp.float32)


def per_device(hidden_in, norm_gain, w_gate, w_up, w_down, expert_ids, gate_weights):
    row_count = hidden_in.shape[0]
    capacity = row_count // 2
    normed = rms_scale(hidden_in, norm_gain[0])
    chosen = expert_ids == 0
    routed = jnp.any(chosen, axis=1)
    own_weight = jnp.sum(jnp.where(chosen, gate_weights, 0.0), axis=1)
    position = jnp.cumsum(routed.astype(jnp.int32)) - 1
    slot_grid = lax.broadcasted_iota(jnp.int32, (capacity, row_count), 0)
    token_grid = lax.broadcasted_iota(jnp.int32, (capacity, row_count), 1)
    picked = (position[None, :] == slot_grid) & routed[None, :]
    source = jnp.sum(jnp.where(picked, token_grid, 0), axis=1)
    filled = jnp.any(picked, axis=1)
    packed = jnp.where(
        filled[:, None], jnp.take(normed, source, axis=0), jnp.zeros_like(normed[:1])
    )
    gate_matrix = w_gate[0]
    up_matrix = w_up[0]
    down_matrix = w_down[0]
    terms = expert_rows(
        lax.all_gather(packed, ("expert", "dp"), axis=0, tiled=True),
        gate_matrix,
        up_matrix,
        down_matrix,
    )
    own_rows = lax.psum_scatter(
        terms.astype(jnp.bfloat16), ("expert", "dp"), scatter_dimension=0, tiled=True
    ).astype(jnp.float32)
    back = jnp.take(own_rows, jnp.clip(position, 0, capacity - 1), axis=0)
    branch = jnp.where(routed[:, None], back, 0.0)
    combined = (hidden_in.astype(jnp.float32) + own_weight[:, None] * branch).astype(jnp.bfloat16)
    return passed_along(combined, "pipe", 1)


def solution(mesh):
    return jax.shard_map(
        per_device,
        mesh=mesh,
        in_specs=(
            P(("pipe", "expert", "dp"), None),
            P("pipe", None),
            P("pipe", None, ("expert", "dp")),
            P("pipe", None, ("expert", "dp")),
            P("pipe", ("expert", "dp"), None),
            P(("pipe", "expert", "dp"), None),
            P(("pipe", "expert", "dp"), None),
        ),
        out_specs=P(("pipe", "expert", "dp"), None),
        check_vma=False,
    )
```

profile of v0, /device:TPU:1, one launch (start us, length us, event | category | flops | bytes accessed | tf_op | source)
XLA Modules:
  0.0 317.8 jit_solution(4532559562658368236)
XLA Ops:
  6.5 0.0 all-gather.2.cloned.1.call-start
  6.5 0.7 fusion.15
  7.2 0.1 copy.10
  7.4 0.2 reduce-window.4
  7.5 0.1 fusion.11
  7.6 0.1 select_reduce_fusion
  7.8 0.1 fusion.13
  7.9 1.8 fusion.5
  9.7 1.9 fusion.7
  11.6 1.0 gather_fusion
  12.6 1.0 select_select_fusion
  13.7 0.0 all-gather.2.cloned.1.call-update
  13.7 0.0 reduce-scatter.2.cloned.1.call-start
  13.7 75.7 %all-gather.2.cloned.1.call-done = bf16[1024,6144]{1,0:T(8,128)(2,1)} async-done(((bf16[64,6144]{1,0:T(8,128)(2,1)}), bf16[1024,6144]{1,0:T(8,128)(2,1)}) %all-gather.2.cloned.1.call-update) | async-done | bytes 12582928 | tf_op jit(solution)/shard_map/all_gather | solution.py:46
  89.4 0.0 copy-start.3
  89.4 11.6 %fusion.1 = f32[1024,512]{1,0:T(8,128)S(1)} fusion(bf16[1024,6144]{1,0:T(8,128)(2,1)} %all-gather.2.cloned.1.call-done, bf16[1,6144,512]{2,1,0:T(8,128)(2,1)} %param.10), kind=kOutput, calls=%fused_computation.4 | convolution fusion | flops 6442450944 | bytes 20971520 | tf_op jit(solution)/shard_map/dot_general | solution.py:21
  101.0 0.0 copy-done.3
  101.0 8.8 %multiply_convert_fusion = bf16[1024,512]{1,0:T(8,128)(2,1)S(1)} fusion(f32[1024,512]{1,0:T(8,128)S(1)} %fusion.1, bf16[1024,6144]{1,0:T(8,128)(2,1)S(1)} %copy-done.3, bf16[1,6144,512]{2,1,0:T(8,128)(2,1)} %param.9), kind=kOutput, calls=%fused_computation.15 | convolution fusion | flops 6445596672 | bytes 22020096 | tf_op jit(solution)/shard_map/dot_general | solution.py:20
  109.8 12.4 %convolution_convert_fusion = bf16[1024,6144]{1,0:T(8,128)(2,1)} fusion(bf16[1024,512]{1,0:T(8,128)(2,1)S(1)} %multiply_convert_fusion, bf16[1,512,6144]{2,1,0:T(8,128)(2,1)} %param.11), kind=kOutput, calls=%fused_computation.2 | convolution fusion | flops 6448742400 | bytes 19922944 | tf_op jit(solution)/shard_map/dot_general | solution.py:23
  122.2 0.0 copy-start.1
  122.2 0.0 copy-start.2
  122.2 0.0 reduce-scatter.2.cloned.1.call-update
  122.2 0.6 copy-done.1
  122.9 0.0 copy-done.2
  122.9 140.6 %reduce-scatter.2.cloned.1.call-done = bf16[64,6144]{1,0:T(8,128)(2,1)} async-done(((bf16[1024,6144]{1,0:T(8,128)(2,1)}), bf16[64,6144]{1,0:T(8,128)(2,1)}) %reduce-scatter.2.cloned.1.call-update) | async-done | bytes 786448 | tf_op jit(solution)/shard_map/reduce_scatter | solution.py:51
  263.5 1.2 convert_element_type.38
  264.7 0.0 copy-start
  264.7 3.2 gather_fusion.1
  267.9 0.0 copy-done
  267.9 2.7 fusion.8
  270.6 2.5 collective-permute-start
  273.1 36.8 %collective-permute-done = bf16[128,6144]{1,0:T(8,128)(2,1)S(1)} collective-permute-done((bf16[128,6144]{1,0:T(8,128)(2,1)S(1)}, bf16[128,6144]{1,0:T(8,128)(2,1)S(1)}, u32[]{:S(2)}, u32[]{:S(2)}) %collective-permute-start) | collective-permute-done | bytes 1572896 | tf_op jit(solution)/shard_map/ppermute | solution.py:10
  309.9 1.1 copy.12
  (8 shorter events, 0.1 us)
Async XLA Ops:
  6.5 82.8 %all-gather.2.cloned.1.call-start = ((), (), s32[]{:S(2)}) async-start(), calls=%async_computation.1 | async-start | bytes 13369344 | tf_op jit(solution)/shard_map/all_gather | solution.py:46
  13.7 249.8 %reduce-scatter.2.cloned.1.call-start = ((), (), s32[]{:S(2)}) async-start(), calls=%async_computation.2 | async-start | bytes 13369344 | tf_op jit(solution)/shard_map/reduce_scatter | solution.py:51
  89.4 11.6 %copy-start.3 = (bf16[1024,6144]{1,0:T(8,128)(2,1)S(1)}, bf16[1024,6144]{1,0:T(8,128)(2,1)}, u32[]{:S(2)}) copy-start(bf16[1024,6144]{1,0:T(8,128)(2,1)} %all-gather.2.cloned.1.call-done) | copy-start | bytes 37748740
  122.2 0.7 copy-start.1
  122.2 0.7 copy-start.2
  264.7 3.2 %copy-start = (bf16[128,6144]{1,0:T(8,128)(2,1)S(1)}, bf16[128,6144]{1,0:T(8,128)(2,1)}, u32[]{:S(2)}) copy-start(bf16[128,6144]{1,0:T(8,128)(2,1)} %param.7) | copy-start | bytes 4718596
  270.6 39.3 %collective-permute-start = (bf16[128,6144]{1,0:T(8,128)(2,1)S(1)}, bf16[128,6144]{1,0:T(8,128)(2,1)S(1)}, u32[]{:S(2)}, u32[]{:S(2)}) collective-permute-start(bf16[128,6144]{1,0:T(8,128)(2,1)S(1)} %fusion.8), channel_id=1, source_target_pairs={{112,0},{0,16},{16,32},{32,48},{48,64},{64,80},{80,96},{96,112},{1... | collective-permute-start | bytes 4718600 | tf_op jit(solution)/shard_map/ppermute | solution.py:10
Sparse Core Ops, SparseCore 0:
  13.8 75.5 all-gather.1
  122.3 141.1 reduce-scatter.1
where the time goes:
time: 318 us
  waiting for transfers between devices  253 us (80%)
  matrix products  32.8 us (10%)
  between operations  13.5 us (4%)
  other arithmetic  9.89 us (3%)
  local copies, waits for them, and re-layouts  6.12 us (2%)
    reduce_scatter x1, waiting for transfers between devices, per_device(): lax.psum_scatter(terms.astype(jnp.bfloat16), ('expert', 'dp'), scatter_di...  141 us
    all_gather x1, waiting for transfers between devices, per_device(): lax.all_gather(packed, ('expert', 'dp'), axis=0, tiled=True)  75.7 us
    ppermute x1, waiting for transfers between devices, passed_along(): return lax.ppermute(block, axis, route)  36.8 us
    dot_general x1, matrix products, expert_rows(): return jnp.dot(hidden, down_matrix, preferred_element_type=jnp.float32)  12.4 us
    dot_general x1, matrix products, expert_rows(): up_values = jnp.dot(normed, up_matrix, preferred_element_type=jnp.float32)  11.6 us
    dot_general x1, matrix products, expert_rows(): gate = jnp.dot(normed, gate_matrix, preferred_element_type=jnp.float32)  8.84 us
  transfers between devices with their start and end apart: 3, of which 3 were waited for; matrix products, arithmetic and copies ran while one was open for 0% of the time, Pallas kernels for 0%

commit v1 on v0

v1 whole, which is shorter than its diff:
```python
import functools

import jax
import jax.numpy as jnp
from jax import lax
from jax.experimental import pallas as pl
from jax.experimental.pallas import tpu as pltpu
from jax.sharding import PartitionSpec as P

MESH = pl.DeviceIdType.MESH
F32 = jnp.float32
BF16 = jnp.bfloat16
CHIPS = 8
MEMBERS = 16


def iota(shape, dim):
    return lax.broadcasted_iota(jnp.int32, shape, dim).astype(F32)


def kernel(
    sections,
    x_hbm, gain, wg_hbm, wu_hbm, wd_hbm, ids, gw,
    out,
    x_v, x_in, route, route_in, counts, wg, wu, wd, packed, slots, pick, place,
    gath, acc_g, acc_u, hid, own, core_out, core_in, opp_out, opp_in,
    near_out, near_in, cross_out, cross_in, back_out, back_in,
    load_sem, cnt_s, cnt_r, a2a_s, a2a_r, gath_s, gath_r, core_s, core_r,
    opp_s, opp_r, near_s, near_r, cross_s, cross_r, back_s, back_r, relay_s, relay_r,
):
    p, c, d = lax.axis_index("pipe"), lax.axis_index("expert"), lax.axis_index("dp")
    y, z = d // 4, d % 4
    me = d * 2 + c
    after, before = lax.rem(p + 1, sections), lax.rem(p + sections - 1, sections)
    tokens, width = x_v.shape
    cap = packed.shape[1]
    part = packed.shape[2]
    half = gath.shape[3]
    rows = 2 * half

    def chip(other_y, step):
        yy = 1 - y if other_y else y
        return yy * 4 + (z + step) % 4

    up, down, across = chip(False, 1), chip(False, 3), chip(True, 0)
    to_up, to_down, to_across = (p, c, up), (p, c, down), (p, c, across)
    to_core = (p, 1 - c, d)

    def remote(src, dst, send, recv, device):
        return pltpu.make_async_remote_copy(
            src_ref=src, dst_ref=dst, send_sem=send, recv_sem=recv,
            device_id=device, device_id_type=MESH,
        )

    load_x = pltpu.make_async_copy(x_hbm, x_v, load_sem.at[0])
    load_g = pltpu.make_async_copy(wg_hbm, wg, load_sem.at[1])
    load_u = pltpu.make_async_copy(wu_hbm, wu, load_sem.at[2])
    load_x.start()

    barrier = pltpu.get_barrier_semaphore()

    def member(i):
        return i % 2, i // 2

    def greet(k, carry):
        e, dd = member((me + k) % MEMBERS)
        pl.semaphore_signal(barrier, inc=1, device_id=(p, e, dd), device_id_type=MESH)
        return carry

    def greet_before(k, carry):
        e, dd = member(k)
        pl.semaphore_signal(barrier, inc=1, device_id=(before, e, dd), device_id_type=MESH)
        return carry

    lax.fori_loop(1, MEMBERS, greet, 0)
    lax.fori_loop(0, MEMBERS, greet_before, 0)

    load_g.start()
    load_u.start()
    loads_d = []
    for e in range(2):
        for j in range(CHIPS):
            cp = pltpu.make_async_copy(
                wd_hbm.at[:, pl.ds((2 * j + e) * part, part)], wd.at[j, e],
                load_sem.at[3 + 2 * j + e],
            )
            cp.start()
            loads_d.append(cp)

    chosen = ids[...] == 0
    routed = jnp.max(jnp.where(chosen, 1.0, 0.0), axis=1, keepdims=True)
    weight = jnp.sum(jnp.where(chosen, gw[...], 0.0), axis=1, keepdims=True)
    routed_b = jnp.broadcast_to(routed, (tokens, tokens))
    tri = jnp.where(iota((tokens, tokens), 0) >= iota((tokens, tokens), 1), 1.0, 0.0)
    rank = jnp.dot(tri.astype(BF16), routed_b.astype(BF16), preferred_element_type=F32)
    lane = iota((tokens, tokens), 1)
    spot = jnp.where((routed_b > 0.5) & (rank - 1.0 == lane), 1.0, 0.0)
    route[...] = jnp.where(lane < cap, spot, jnp.broadcast_to(weight, (tokens, tokens)))
    spot_t = spot.T[:cap].astype(BF16)
    counts[me] = jnp.dot(
        jnp.ones((8, tokens), BF16), routed_b.astype(BF16), preferred_element_type=F32
    )

    load_x.wait()

    def squares(j, total):
        v = x_v[:, pl.ds(pl.multiple_of(j * part, 128), part)].astype(F32)
        return total + jnp.sum(v * v, axis=1, keepdims=True)

    total = lax.fori_loop(0, MEMBERS, squares, jnp.zeros((tokens, 1), F32))
    scale = lax.rsqrt(total / width + 1e-05)

    def pack(j, carry):
        at = pl.ds(pl.multiple_of(j * part, 128), part)
        n = (x_v[:, at].astype(F32) * scale * gain[:, at]).astype(BF16)
        packed[j] = jnp.dot(spot_t, n, preferred_element_type=F32).astype(BF16)
        return carry

    lax.fori_loop(0, MEMBERS, pack, 0)
    slots[me] = packed[me]

    pl.semaphore_wait(barrier, 2 * MEMBERS - 1)

    def count_copy(k):
        i = (me + k) % MEMBERS
        e, dd = member(i)
        return remote(counts.at[me], counts.at[me], cnt_s.at[i], cnt_r.at[me], (p, e, dd))

    def count_from(k):
        i = (me + k) % MEMBERS
        return remote(counts.at[i], counts.at[i], cnt_s.at[i], cnt_r.at[i], to_core)

    def slot_copy(k):
        i = (me + k) % MEMBERS
        e, dd = member(i)
        return remote(packed.at[i], slots.at[me], a2a_s.at[i], a2a_r.at[me], (p, e, dd))

    def slot_from(k):
        i = (me + k) % MEMBERS
        return remote(packed.at[i], slots.at[i], a2a_s.at[i], a2a_r.at[i], to_core)

    def loop(first, last, body):
        def step(k, carry):
            body(k)
            return carry

        lax.fori_loop(first, last, step, 0)

    loop(1, MEMBERS, lambda k: count_copy(k).start())
    loop(1, MEMBERS, lambda k: slot_copy(k).start())
    relay_route = remote(route, route_in, relay_s.at[0], relay_r.at[0], (after, c, d))
    relay_route.start()
    loop(1, MEMBERS, lambda k: count_from(k).wait_recv())

    off = jnp.zeros((1, 128), F32)
    lane1 = iota((1, 128), 1)
    row_i = iota((rows, 128), 0)
    s_i, r_i = iota((cap, rows), 0), iota((cap, rows), 1)
    for q in range(MEMBERS // 2):
        n0, n1 = counts[2 * q][0:1], counts[2 * q + 1][0:1]
        high = lane1 - cap
        target = jnp.where(
            lane1 < cap,
            jnp.where(lane1 < n0, off + lane1, -1.0),
            jnp.where(high < n1, off + n0 + high, -1.0),
        )
        pick[:, q * 128:(q + 1) * 128] = jnp.where(row_i == target, 1.0, 0.0).astype(BF16)
        for t, (o, n) in enumerate(((off, n0), (off + n0, n1))):
            hit = (r_i - s_i == o[:, 0:1]) & (s_i < n[:, 0:1])
            place[(2 * q + t) * cap:(2 * q + t + 1) * cap] = jnp.where(hit, 1.0, 0.0).astype(BF16)
        off = off + n0 + n1

    loop(1, MEMBERS, lambda k: slot_from(k).wait_recv())
    all_slots = slots[...].reshape(MEMBERS * cap, part)
    for h in range(2):
        gath[d, c, h] = jnp.dot(
            pick[h * half:(h + 1) * half], all_slots, preferred_element_type=F32
        ).astype(BF16)

    sends = []

    def piece(j, e, h):
        return gath.at[j, e, h], gath_r.at[j, e, h]

    def send_piece(j, h, device):
        ref, sem = piece(j, c, h)
        cp = remote(ref, ref, gath_s.at[len(sends)], sem, device)
        cp.start()
        sends.append(cp)

    def wait_piece(j, e, h):
        ref, sem = piece(j, e, h)
        remote(ref, ref, gath_s.at[0], sem, to_core).wait_recv()

    def multiply(j, first=False):
        for h in range(2):
            wait_piece(j, 1 - c, h)

        def tile(n):
            at = pl.ds(pl.multiple_of(n * 256, 256), 256)
            a = jnp.concatenate(
                [
                    jnp.concatenate([gath[j, e, h] for e in range(2)], axis=1)
                    for h in range(2)
                ],
                axis=0,
            )
            for w, acc in ((wg, acc_g), (wu, acc_u)):
                v = jnp.dot(a, w[j, :, at], preferred_element_type=F32)
                if first:
                    acc[:, at] = v
                else:
                    acc[:, at] += v

        loop(0, acc_g.shape[1] // 256, tile)

    send_piece(d, 0, to_up)
    send_piece(d, 1, to_down)
    send_piece(d, 0, to_across)
    send_piece(d, 1, to_across)
    send_piece(d, 1, to_up)
    send_piece(d, 0, to_down)
    send_piece(d, 0, to_core)
    send_piece(d, 1, to_core)

    load_g.wait()
    load_u.wait()
    multiply(d, first=True)

    wait_piece(down, c, 0)
    send_piece(down, 0, to_up)
    send_piece(down, 0, to_core)
    wait_piece(up, c, 1)
    send_piece(up, 1, to_down)
    send_piece(up, 1, to_core)
    wait_piece(across, c, 0)
    send_piece(across, 0, to_up)
    send_piece(across, 0, to_core)
    wait_piece(across, c, 1)
    send_piece(across, 1, to_down)
    send_piece(across, 1, to_up)
    send_piece(across, 0, to_down)
    send_piece(across, 1, to_core)
    relay_x = remote(x_v, x_in, relay_s.at[1], relay_r.at[1], (after, c, d))
    relay_x.start()
    wait_piece(down, c, 1)
    send_piece(down, 1, to_core)
    wait_piece(up, c, 0)
    send_piece(up, 0, to_core)
    multiply(across)
    multiply(down)
    multiply(up)
    aup, adown = chip(True, 1), chip(True, 3)
    wait_piece(adown, c, 0)
    send_piece(adown, 0, to_up)
    send_piece(adown, 0, to_core)
    wait_piece(aup, c, 1)
    send_piece(aup, 1, to_down)
    send_piece(aup, 1, to_core)
    wait_piece(adown, c, 1)
    send_piece(adown, 1, to_core)
    wait_piece(aup, c, 0)
    send_piece(aup, 0, to_core)
    far, afar = chip(False, 2), chip(True, 2)
    wait_piece(far, c, 0)
    send_piece(far, 0, to_core)
    wait_piece(far, c, 1)
    send_piece(far, 1, to_core)
    multiply(adown)
    multiply(aup)
    multiply(far)
    wait_piece(afar, c, 0)
    send_piece(afar, 0, to_core)
    wait_piece(afar, c, 1)
    send_piece(afar, 1, to_core)
    multiply(afar)

    def activate(n):
        at = pl.ds(pl.multiple_of(n * 128, 128), 128)
        g = acc_g[at]
        hid[at] = (g / (1.0 + jnp.exp(-g)) * acc_u[at]).astype(BF16)

    loop(0, rows // 128, activate)
    for cp in loads_d:
        cp.wait()

    order = [(o, s) for o in (True, False) for s in (2, 1, 3, 0)]
    core_copies = []

    def project(k):
        j = chip(*order[k])
        a = hid[...]
        core_out[k] = jnp.dot(a, wd[j, 1 - c], preferred_element_type=F32).astype(BF16)
        cp = remote(core_out.at[k], core_in.at[k], core_s.at[k], core_r.at[k], to_core)
        cp.start()
        core_copies.append(cp)
        own[k] = jnp.dot(a, wd[j, c], preferred_element_type=F32)

    def both(k, h):
        at = pl.ds(h * half, half)
        return own[k, at] + core_in[k, at].astype(F32)

    others = []

    def pass_on(src, dst, send, recv, device):
        cp = remote(src, dst, send, recv, device)
        cp.start()
        others.append(cp)

    def send_far(g):
        core_copies[4 * g].wait_recv()
        for h, device in ((0, to_up), (1, to_down)):
            opp_out[g, h] = both(4 * g, h).astype(BF16)
            pass_on(opp_out.at[g, h], opp_in.at[g, h], opp_s.at[g, h], opp_r.at[g, h], device)

    def send_near(g, way, h, add):
        k = 4 * g + 1 + way
        v = both(k, h)
        if add:
            v = v + opp_in[g, h].astype(F32)
        near_out[g, way, h] = v.astype(BF16)
        pass_on(
            near_out.at[g, way, h], near_in.at[g, way, h],
            near_s.at[g, way, h], near_r.at[g, way, h], to_down if way else to_up,
        )

    def wait_far(g, h):
        remote(
            opp_out.at[g, h], opp_in.at[g, h], opp_s.at[g, h], opp_r.at[g, h], to_up
        ).wait_recv()

    def wait_near(g):
        for way in range(2):
            for h in range(2):
                remote(
                    near_out.at[g, way, h], near_in.at[g, way, h],
                    near_s.at[g, way, h], near_r.at[g, way, h], to_up,
                ).wait_recv()

    def collect(g, h):
        return both(4 * g + 3, h) + near_in[g, 0, h].astype(F32) + near_in[g, 1, h].astype(F32)

    def dependent(g):
        wait_far(g, 0)
        send_near(g, 0, 0, True)
        wait_far(g, 1)
        send_near(g, 1, 1, True)

    project(0)
    project(1)
    send_far(0)
    project(2)
    core_copies[1].wait_recv()
    send_near(0, 0, 1, False)
    project(3)
    core_copies[2].wait_recv()
    send_near(0, 1, 0, False)
    project(4)
    project(5)
    dependent(0)
    send_far(1)
    project(6)
    core_copies[5].wait_recv()
    send_near(1, 0, 1, False)
    project(7)
    core_copies[6].wait_recv()
    send_near(1, 1, 0, False)
    dependent(1)
    core_copies[3].wait_recv()
    wait_near(0)
    for h in range(2):
        cross_out[h] = collect(0, h).astype(BF16)
    cross = remote(cross_out, cross_in, cross_s, cross_r, to_across)
    cross.start()
    core_copies[7].wait_recv()
    wait_near(1)
    cross.wait_recv()
    final = jnp.concatenate(
        [(collect(1, h) + cross_in[h].astype(F32)).astype(BF16) for h in range(2)], axis=0
    )

    def unpack(i):
        at = pl.ds(pl.multiple_of(i * cap, cap), cap)
        back_out[i] = jnp.dot(place[at], final, preferred_element_type=F32).astype(BF16)
        e, dd = member(i)
        remote(
            back_out.at[i], back_in.at[me], back_s.at[i], back_r.at[me], (after, e, dd)
        ).start()

    loop(0, MEMBERS, unpack)

    relay_route.wait_recv()
    relay_x.wait_recv()
    spread = route_in[:, :cap].astype(BF16)
    scale_in = route_in[:, cap:cap + 1]

    def back_from(k):
        return remote(back_out.at[k], back_in.at[k], back_s.at[k], back_r.at[k], to_core)

    def finish(k):
        back_from(k).wait_recv()
        at = pl.ds(pl.multiple_of(k * part, 128), part)
        term = jnp.dot(spread, back_in[k], preferred_element_type=F32)
        out[:, at] = (x_in[:, at].astype(F32) + scale_in * term).astype(BF16)

    loop(0, MEMBERS, finish)

    loop(1, MEMBERS, lambda k: count_copy(k).wait_send())
    loop(1, MEMBERS, lambda k: slot_copy(k).wait_send())
    loop(0, MEMBERS, lambda k: back_from(k).wait_send())
    for cp in sends + core_copies + others + [cross, relay_route, relay_x]:
        cp.wait_send()


def solution(mesh):
    sections = mesh.shape["pipe"]

    def per_device(hidden_in, norm_gain, w_gate, w_up, w_down, expert_ids, gate_weights):
        tokens, width = hidden_in.shape
        ff = w_gate.shape[2]
        cap = tokens // 2
        rows = MEMBERS * cap // 2
        half = rows // 2
        part = width // MEMBERS
        vmem = pltpu.VMEM
        dma = pltpu.SemaphoreType.DMA
        any_space = pl.BlockSpec(memory_space=pl.ANY)
        in_vmem = pl.BlockSpec(memory_space=pltpu.VMEM)
        return pl.pallas_call(
            functools.partial(kernel, sections),
            out_shape=jax.ShapeDtypeStruct((tokens, width), BF16),
            in_specs=[any_space, in_vmem, any_space, any_space, any_space, in_vmem, in_vmem],
            out_specs=in_vmem,
            scratch_shapes=[
                vmem((tokens, width), BF16),
                vmem((tokens, width), BF16),
                vmem((tokens, tokens), F32),
                vmem((tokens, tokens), F32),
                vmem((MEMBERS, 8, 128), F32),
                vmem((CHIPS, 2 * part, ff), BF16),
                vmem((CHIPS, 2 * part, ff), BF16),
                vmem((CHIPS, 2, ff, part), BF16),
                vmem((MEMBERS, cap, part), BF16),
                vmem((MEMBERS, cap, part), BF16),
                vmem((rows, MEMBERS * cap), BF16),
                vmem((MEMBERS * cap, rows), BF16),
                vmem((CHIPS, 2, 2, half, part), BF16),
                vmem((rows, ff), F32),
                vmem((rows, ff), F32),
                vmem((rows, ff), BF16),
                vmem((CHIPS, rows, part), F32),
                vmem((CHIPS, rows, part), BF16),
                vmem((CHIPS, rows, part), BF16),
                vmem((2, 2, half, part), BF16),
                vmem((2, 2, half, part), BF16),
                vmem((2, 2, 2, half, part), BF16),
                vmem((2, 2, 2, half, part), BF16),
                vmem((2, half, part), BF16),
                vmem((2, half, part), BF16),
                vmem((MEMBERS, cap, part), BF16),
                vmem((MEMBERS, cap, part), BF16),
                dma((19,)),
                dma((MEMBERS,)), dma((MEMBERS,)),
                dma((MEMBERS,)), dma((MEMBERS,)),
                dma((32,)), dma((CHIPS, 2, 2)),
                dma((CHIPS,)), dma((CHIPS,)),
                dma((2, 2)), dma((2, 2)),
                dma((2, 2, 2)), dma((2, 2, 2)),
                dma, dma,
                dma((MEMBERS,)), dma((MEMBERS,)),
                dma((2,)), dma((2,)),
            ],
            compiler_params=pltpu.CompilerParams(
                collective_id=0, has_side_effects=True, vmem_limit_bytes=62 * 2**20
            ),
            name="routed_block",
        )(
            hidden_in,
            norm_gain,
            w_gate.reshape(CHIPS, 2 * part, ff),
            w_up.reshape(CHIPS, 2 * part, ff),
            w_down.reshape(ff, width),
            expert_ids,
            gate_weights,
        )

    return jax.shard_map(
        per_device,
        mesh=mesh,
        in_specs=(
            P(("pipe", "expert", "dp"), None),
            P("pipe", None),
            P("pipe", None, ("expert", "dp")),
            P("pipe", None, ("expert", "dp")),
            P("pipe", ("expert", "dp"), None),
            P(("pipe", "expert", "dp"), None),
            P(("pipe", "expert", "dp"), None),
        ),
        out_specs=P(("pipe", "expert", "dp"), None),
        check_vma=False,
    )
```

time: 318 us -> 128 us (0.40)
  the two profiles are of different devices: /device:TPU:1 before, /device:TPU:105 now
where the time goes in v1:
time: 128 us
  Pallas kernels  122 us (95%)
  local copies, waits for them, and re-layouts  5.5 us (4%)
    pallas_call x1, Pallas kernels, per_device(): pl.pallas_call(functools.partial(kernel, sections), out_shape=jax.ShapeDt...  122 us
    unnamed x3, local copies, waits for them, and re-layouts  5.5 us

profile of v1, /device:TPU:105, one launch (start us, length us, event | category | flops | bytes accessed | tf_op | source)
XLA Modules:
  0.0 127.7 jit_solution(9920201190093469267)
XLA Ops:
  0.0 1.4 %copy.8.ids = s32[128,2]{1,0:T(8,128)} copy(s32[128,2]{0,1:T(2,128)} %param.12) | data formatting | bytes 2048 | tf_op args[5]
  1.4 1.4 %copy.9.gw = f32[128,2]{1,0:T(8,128)} copy(f32[128,2]{0,1:T(2,128)} %param.13) | data formatting | bytes 2048 | tf_op args[6]
  2.8 122.2 %routed_block.1 = bf16[128,6144]{1,0:T(8,128)(2,1)} custom-call(bf16[128,6144]{1,0:T(8,128)(2,1)} %x_hbm.1, f32[1,6144]{1,0:T(1,128)} %gain.1, bf16[8,768,512]{2,1,0:T(8,128)(2,1)} %bitcast.3, bf16[8,768,512]{2,1,0:T(8,128)(2,1)} %bitcast.4, bf16[512,6144]{1,0:T(8,128)(2,1)} %bitcast.5, s32[128,2]{1,0:T(8,128)} %copy.8.ids, f32[128,2]{1,0:T(8,128)} %copy.9.gw), custom_call_target="tpu_custom_call" | custom-call | tf_op jit(solution)/shard_map/routed_block/pallas_call | solution.py:429
  125.0 2.7 %copy.11 = bf16[128,6144]{1,0:T(8,128)(2,1)} copy(bf16[128,6144]{1,0:T(8,128)(2,1)} %routed_block.1) | data formatting | bytes 3145728

commit v2 on v0

v2 whole, which is shorter than its diff:
```python
import functools

import jax
import jax.numpy as jnp
from jax import lax
from jax.experimental import pallas as pl
from jax.experimental.pallas import tpu as pltpu
from jax.sharding import PartitionSpec as P

MESH = pl.DeviceIdType.MESH
F32 = jnp.float32
BF16 = jnp.bfloat16
CHIPS = 8
MEMBERS = 16
LANES = 128


def iota(shape, dim):
    return lax.broadcasted_iota(jnp.int32, shape, dim).astype(F32)


def kernel(
    sections,
    x_hbm, gain, wg_hbm, wu_hbm, wd_hbm, ids, gw,
    out,
    x_v, x_in, route, route_in, counts, counts_in, wg, wu, wd, packed, slots, pick, place,
    gath, acc_g, acc_u, hid, own, core_out, core_in, opp_out, opp_in,
    near_out, near_in, sum_out, sum_in, back_out, back_in,
    load_sem, cnt_s, cnt_r, a2a_s, a2a_r, gath_s, gath_r, core_s, core_r,
    opp_s, opp_r, near_s, near_r, sum_s, sum_r, back_s, back_r, relay_s, relay_r,
):
    p, c, d = lax.axis_index("pipe"), lax.axis_index("expert"), lax.axis_index("dp")
    y, z = d // 4, d % 4
    me = d * 2 + c
    after, before = lax.rem(p + 1, sections), lax.rem(p + sections - 1, sections)
    tokens, width = x_v.shape
    cap = packed.shape[1]
    part = packed.shape[2]
    half = gath.shape[3]
    rows = 2 * half
    strips = part // LANES
    cuts = ((0, LANES), (LANES, part - LANES))

    def chip(other_y, step):
        yy = 1 - y if other_y else y
        return yy * 4 + (z + step) % 4

    up, down, across = chip(False, 1), chip(False, 3), chip(True, 0)
    to_up, to_down, to_across = (p, c, up), (p, c, down), (p, c, across)
    to_core = (p, 1 - c, d)

    def remote(src, dst, send, recv, device):
        return pltpu.make_async_remote_copy(
            src_ref=src, dst_ref=dst, send_sem=send, recv_sem=recv,
            device_id=device, device_id_type=MESH,
        )

    def loop(first, last, body):
        def step(k, carry):
            body(k)
            return carry

        lax.fori_loop(first, last, step, 0)

    def member(k):
        i = (me + k) % MEMBERS
        return i, (p, i % 2, i // 2)

    load_x = pltpu.make_async_copy(x_hbm, x_v, load_sem.at[0])
    load_g = pltpu.make_async_copy(wg_hbm, wg, load_sem.at[1])
    load_u = pltpu.make_async_copy(wu_hbm, wu, load_sem.at[2])
    load_x.start()

    barrier = pltpu.get_barrier_semaphore()

    def greet(device):
        pl.semaphore_signal(barrier, inc=1, device_id=device, device_id_type=MESH)

    loop(1, MEMBERS, lambda k: greet(member(k)[1]))
    greet((before, c, d))
    greet((before, c, across))

    square = (tokens, tokens)
    chosen = ids[...] == 0
    routed = jnp.max(jnp.where(chosen, 1.0, 0.0), axis=0, keepdims=True)
    weight = jnp.sum(jnp.where(chosen, gw[...], 0.0), axis=0, keepdims=True)
    routed_b = jnp.broadcast_to(routed, square)
    tri = jnp.where(iota(square, 0) <= iota(square, 1), 1.0, 0.0).astype(BF16)
    rank = jnp.dot(routed_b.astype(BF16), tri, preferred_element_type=F32)
    spot = jnp.where((routed_b > 0.5) & (rank - 1.0 == iota(square, 0)), 1.0, 0.0)
    spot_t = spot[:cap].astype(BF16)
    route[...] = jnp.where(
        iota(square, 1) < cap, spot.T, jnp.broadcast_to(weight, square).T
    )
    counts[me] = jnp.dot(
        routed_b[:8].astype(BF16), jnp.ones(square, BF16), preferred_element_type=F32
    )

    load_x.wait()
    load_g.start()
    load_u.start()
    loads_d = []
    for j in range(CHIPS):
        for e in range(2):
            cp = pltpu.make_async_copy(
                wd_hbm.at[:, pl.ds((2 * j + e) * part, part)], wd.at[j, e],
                load_sem.at[3 + 2 * j + e],
            )
            cp.start()
            loads_d.append(cp)

    def squares(j, total):
        for t in range(strips):
            at = pl.ds(pl.multiple_of(j * part + t * LANES, LANES), LANES)
            v = x_v[:, at].astype(F32)
            total = total + v * v
        return total

    total = lax.fori_loop(0, MEMBERS, squares, jnp.zeros((tokens, LANES), F32))
    scale = lax.rsqrt(jnp.sum(total, axis=1, keepdims=True) / width + 1e-05)

    def pack(j, q):
        start, size = cuts[q]
        for t in range(4):
            i = j * 4 + t
            at = pl.ds(pl.multiple_of(i * part + start, LANES), size)
            n = (x_v[:, at].astype(F32) * scale * gain[:, at]).astype(BF16)
            packed[i, :, start:start + size] = jnp.dot(
                spot_t, n, preferred_element_type=F32
            ).astype(BF16)

    loop(0, MEMBERS // 4, lambda j: pack(j, 0))
    pl.semaphore_wait(barrier, MEMBERS + 1)

    def count_copy(k):
        i, device = member(k)
        return remote(counts.at[me], counts.at[me], cnt_s.at[i], cnt_r.at[me], device)

    def count_from(k):
        i = member(k)[0]
        return remote(counts.at[i], counts.at[i], cnt_s.at[i], cnt_r.at[i], to_core)

    def slot_copy(k, q):
        i, device = member(k)
        at = pl.ds(*cuts[q])
        return remote(
            packed.at[i, :, at], slots.at[me, :, at], a2a_s.at[q, i], a2a_r.at[q, me], device
        )

    def slot_from(k, q):
        i = member(k)[0]
        at = pl.ds(*cuts[q])
        return remote(
            packed.at[i, :, at], slots.at[i, :, at], a2a_s.at[q, i], a2a_r.at[q, i], to_core
        )

    loop(1, MEMBERS, lambda k: count_copy(k).start())

    loop(1, MEMBERS, lambda k: slot_copy(k, 0).start())
    loop(0, MEMBERS // 4, lambda j: pack(j, 1))
    loop(1, MEMBERS, lambda k: slot_copy(k, 1).start())
    slots[me] = packed[me]
    loop(1, MEMBERS, lambda k: count_from(k).wait_recv())
    counterpart = (after, c, d)
    relay_route = remote(route, route_in, relay_s.at[0], relay_r.at[0], counterpart)
    relay_route.start()
    relay_counts = remote(counts, counts_in, relay_s.at[1], relay_r.at[1], counterpart)
    relay_counts.start()

    off = jnp.zeros((1, LANES), F32)
    lane1 = iota((1, LANES), 1)
    high = lane1 - cap
    row_i = iota((rows, LANES), 0)
    for q in range(MEMBERS // 2):
        n0, n1 = counts[2 * q][0:1], counts[2 * q + 1][0:1]
        target = jnp.where(
            lane1 < cap,
            jnp.where(lane1 < n0, off + lane1, -1.0),
            jnp.where(high < n1, off + n0 + high, -1.0),
        )
        pick[:, q * LANES:(q + 1) * LANES] = jnp.where(row_i == target, 1.0, 0.0).astype(BF16)
        off = off + n0 + n1

    sends = []

    def piece(j, e, h, q):
        return gath.at[j, e, h, :, pl.ds(*cuts[q])], gath_r.at[j, e, h, q]

    def send_piece(j, h, q, device):
        ref, sem = piece(j, c, h, q)
        cp = remote(ref, ref, gath_s.at[len(sends)], sem, device)
        cp.start()
        sends.append(cp)

    def wait_piece(j, e, h, q):
        ref, sem = piece(j, e, h, q)
        remote(ref, ref, gath_s.at[0], sem, to_core).wait_recv()

    def multiply(j, q, first=False):
        start, size = cuts[q]
        for h in range(2):
            wait_piece(j, 1 - c, h, q)

        def tile(n):
            at = pl.ds(pl.multiple_of(n * 256, 256), 256)
            cols = slice(start, start + size)
            a = jnp.concatenate(
                [
                    jnp.concatenate([gath[j, e, h, :, cols] for e in range(2)], axis=1)
                    for h in range(2)
                ],
                axis=0,
            )
            for w, acc in ((wg, acc_g), (wu, acc_u)):
                b = jnp.concatenate([w[j, e, cols, at] for e in range(2)], axis=0)
                v = jnp.dot(a, b, preferred_element_type=F32)
                if first:
                    acc[:, at] = v
                else:
                    acc[:, at] += v

        loop(0, acc_g.shape[1] // 256, tile)

    def to_z(j, q, first):
        if first:
            send_piece(j, 0, q, to_up)
            send_piece(j, 1, q, to_down)
        else:
            send_piece(j, 1, q, to_up)
            send_piece(j, 0, q, to_down)

    def forward(below, above, q):
        wait_piece(below, c, 0, q)
        send_piece(below, 0, q, to_up)
        send_piece(below, 0, q, to_core)
        wait_piece(above, c, 1, q)
        send_piece(above, 1, q, to_down)
        send_piece(above, 1, q, to_core)

    def rest(below, above, q):
        wait_piece(below, c, 1, q)
        send_piece(below, 1, q, to_core)
        wait_piece(above, c, 0, q)
        send_piece(above, 0, q, to_core)

    def from_across(q):
        for h in range(2):
            wait_piece(across, c, h, q)
        to_z(across, q, True)
        to_z(across, q, False)
        for h in range(2):
            send_piece(across, h, q, to_core)

    def from_far(j, q):
        for h in range(2):
            wait_piece(j, c, h, q)
            send_piece(j, h, q, to_core)

    for q, (start, size) in enumerate(cuts):
        loop(1, MEMBERS, lambda k: slot_from(k, q).wait_recv())
        all_slots = slots[:, :, start:start + size].reshape(MEMBERS * cap, size)
        for h in range(2):
            gath[d, c, h, :, start:start + size] = jnp.dot(
                pick[h * half:(h + 1) * half], all_slots, preferred_element_type=F32
            ).astype(BF16)
        to_z(d, q, True)
        send_piece(d, 0, q, to_across)
        send_piece(d, 1, q, to_across)
        to_z(d, q, False)
        send_piece(d, 0, q, to_core)
        send_piece(d, 1, q, to_core)

    aup, adown, far, afar = chip(True, 1), chip(True, 3), chip(False, 2), chip(True, 2)
    load_g.wait()
    load_u.wait()
    multiply(d, 0, first=True)
    forward(down, up, 0)
    from_across(0)
    rest(down, up, 0)

    relay_counts.wait_recv()
    off = jnp.zeros((1, LANES), F32)
    s_i, r_i = iota((cap, rows), 0), iota((cap, rows), 1)
    for i in range(MEMBERS):
        n = counts_in[i][0:1]
        hit = (r_i - s_i == off[:, 0:1]) & (s_i < n[:, 0:1])
        place[i * cap:(i + 1) * cap] = jnp.where(hit, 1.0, 0.0).astype(BF16)
        off = off + n

    multiply(d, 1)
    multiply(across, 0)
    forward(down, up, 1)
    multiply(down, 0)
    multiply(up, 0)
    from_across(1)
    relay_x = remote(x_v, x_in, relay_s.at[2], relay_r.at[2], counterpart)
    relay_x.start()
    loop(1, MEMBERS, lambda k: count_copy(k).wait_send())
    for q in range(2):
        loop(1, MEMBERS, lambda k: slot_copy(k, q).wait_send())
    forward(adown, aup, 0)
    multiply(across, 1)
    rest(adown, aup, 0)
    rest(down, up, 1)
    multiply(down, 1)
    multiply(up, 1)
    multiply(adown, 0)
    multiply(aup, 0)
    from_far(far, 0)
    forward(adown, aup, 1)
    from_far(far, 1)
    multiply(far, 0)
    multiply(far, 1)
    rest(adown, aup, 1)
    from_far(afar, 0)
    multiply(adown, 1)
    multiply(aup, 1)
    multiply(afar, 0)
    from_far(afar, 1)
    multiply(afar, 1)

    def activate(n):
        at = pl.ds(pl.multiple_of(n * 128, 128), 128)
        g = acc_g[at]
        hid[at] = (g / (1.0 + jnp.exp(-g)) * acc_u[at]).astype(BF16)

    loop(0, rows // 128, activate)
    for cp in loads_d:
        cp.wait()

    order = [(o, s) for o in (True, False) for s in (2, 1, 3, 0)]
    core_copies = {}
    others = []

    def project(q, k):
        j = chip(*order[k])
        cols = slice(q * LANES, (q + 1) * LANES)
        w = jnp.concatenate([wd[j, 1 - c, :, cols], wd[j, c, :, cols]], axis=1)
        v = jnp.dot(hid[...], w, preferred_element_type=F32)
        core_out[q, k] = v[:, :LANES].astype(BF16)
        cp = remote(
            core_out.at[q, k], core_in.at[q, k], core_s.at[q, k], core_r.at[q, k], to_core
        )
        cp.start()
        core_copies[q, k] = cp
        own[q, k] = v[:, LANES:]

    def both(q, k, h):
        at = pl.ds(h * half, half)
        return own[q, k, at] + core_in[q, k, at].astype(F32)

    def pass_on(src, dst, send, recv, device):
        cp = remote(src, dst, send, recv, device)
        cp.start()
        others.append(cp)

    def send_far(q, g):
        core_copies[q, 4 * g].wait_recv()
        for h, device in ((0, to_up), (1, to_down)):
            opp_out[q, g, h] = both(q, 4 * g, h).astype(BF16)
            pass_on(
                opp_out.at[q, g, h], opp_in.at[q, g, h],
                opp_s.at[q, g, h], opp_r.at[q, g, h], device,
            )

    def send_near(q, g, way, h, add):
        v = both(q, 4 * g + 1 + way, h)
        if add:
            v = v + opp_in[q, g, h].astype(F32)
        near_out[q, g, way, h] = v.astype(BF16)
        pass_on(
            near_out.at[q, g, way, h], near_in.at[q, g, way, h],
            near_s.at[q, g, way, h], near_r.at[q, g, way, h], to_down if way else to_up,
        )

    def free_near(q, g):
        for way, h in ((0, 1), (1, 0)):
            core_copies[q, 4 * g + 1 + way].wait_recv()
            send_near(q, g, way, h, False)

    def independent(q):
        for g in range(2):
            send_far(q, g)
        for g in range(2):
            free_near(q, g)

    def dependent(q):
        for g in range(2):
            for way, h in ((0, 0), (1, 1)):
                remote(
                    opp_out.at[q, g, h], opp_in.at[q, g, h],
                    opp_s.at[q, g, h], opp_r.at[q, g, h], to_up,
                ).wait_recv()
                send_near(q, g, way, h, True)

    def collect(q):
        for g in range(2):
            core_copies[q, 4 * g + 3].wait_recv()
            for way in range(2):
                for h in range(2):
                    remote(
                        near_out.at[q, g, way, h], near_in.at[q, g, way, h],
                        near_s.at[q, g, way, h], near_r.at[q, g, way, h], to_up,
                    ).wait_recv()
            for h in range(2):
                sum_out[q, g, h * half:(h + 1) * half] = (
                    both(q, 4 * g + 3, h)
                    + near_in[q, g, 0, h].astype(F32)
                    + near_in[q, g, 1, h].astype(F32)
                ).astype(BF16)
            pass_on(
                sum_out.at[q, g], sum_in.at[q, y], sum_s.at[q, g], sum_r.at[q, y],
                (after, c, d if g else across),
            )

    def back_copy(k, q):
        i, device = member(k)
        return remote(
            back_out.at[q, i], back_in.at[q, me], back_s.at[q, i], back_r.at[q, me], device
        )

    def back_from(k, q):
        i = member(k)[0]
        return remote(
            back_out.at[q, i], back_in.at[q, i], back_s.at[q, i], back_r.at[q, i], to_core
        )

    def unpack(q):
        for t in range(2):
            remote(
                sum_out.at[q, t], sum_in.at[q, t], sum_s.at[q, t], sum_r.at[q, t], to_core
            ).wait_recv()
        final = (sum_in[q, 0].astype(F32) + sum_in[q, 1].astype(F32)).astype(BF16)
        back_out[q] = (
            jnp.dot(place[...], final, preferred_element_type=F32)
            .astype(BF16)
            .reshape(MEMBERS, cap, LANES)
        )
        loop(1, MEMBERS, lambda k: back_copy(k, q).start())
        back_in[q, me] = back_out[q, me]

    def finish(q):
        spread = route_in[:, :cap].astype(BF16)
        scale_in = route_in[:, cap:cap + 1]
        loop(1, MEMBERS, lambda k: back_from(k, q).wait_recv())

        for k in range(0, MEMBERS, 2):
            pair = jnp.concatenate([back_in[q, k], back_in[q, k + 1]], axis=1)
            term = scale_in * jnp.dot(spread, pair, preferred_element_type=F32)
            for t in range(2):
                start = (k + t) * part + q * LANES
                at = slice(start, start + LANES)
                v = x_in[:, at].astype(F32) + term[:, t * LANES:(t + 1) * LANES]
                out[:, at] = v.astype(BF16)

    def projects(q):
        for k in (0, 4, 1, 2, 5, 6, 3, 7):
            project(q, k)

    project(0, 0)
    project(0, 4)
    project(0, 1)
    project(0, 2)
    send_far(0, 0)
    project(0, 5)
    send_far(0, 1)
    project(0, 6)
    free_near(0, 0)
    project(0, 3)
    project(0, 7)
    free_near(0, 1)
    projects(1)
    dependent(0)
    independent(1)
    projects(2)
    collect(0)
    dependent(1)
    independent(2)
    collect(1)
    dependent(2)
    unpack(0)
    collect(2)
    unpack(1)
    relay_route.wait_recv()
    relay_x.wait_recv()
    finish(0)
    unpack(2)
    finish(1)
    for cp in sends + list(core_copies.values()) + others:
        cp.wait_send()
    for cp in (relay_route, relay_counts, relay_x):
        cp.wait_send()
    for q in range(2):
        loop(1, MEMBERS, lambda k: back_copy(k, q).wait_send())
    finish(2)
    loop(1, MEMBERS, lambda k: back_copy(k, 2).wait_send())


def solution(mesh):
    sections = mesh.shape["pipe"]

    def per_device(hidden_in, norm_gain, w_gate, w_up, w_down, expert_ids, gate_weights):
        tokens, width = hidden_in.shape
        ff = w_gate.shape[2]
        cap = tokens // 2
        rows = MEMBERS * cap // 2
        half = rows // 2
        part = width // MEMBERS
        strips = part // LANES
        vmem = pltpu.VMEM
        dma = pltpu.SemaphoreType.DMA
        any_space = pl.BlockSpec(memory_space=pl.ANY)
        in_vmem = pl.BlockSpec(memory_space=pltpu.VMEM)
        return pl.pallas_call(
            functools.partial(kernel, sections),
            out_shape=jax.ShapeDtypeStruct((tokens, width), BF16),
            in_specs=[any_space, in_vmem, any_space, any_space, any_space, in_vmem, in_vmem],
            out_specs=in_vmem,
            scratch_shapes=[
                vmem((tokens, width), BF16),
                vmem((tokens, width), BF16),
                vmem((tokens, tokens), F32),
                vmem((tokens, tokens), F32),
                vmem((MEMBERS, 8, LANES), F32),
                vmem((MEMBERS, 8, LANES), F32),
                vmem((CHIPS, 2, part, ff), BF16),
                vmem((CHIPS, 2, part, ff), BF16),
                vmem((CHIPS, 2, ff, part), BF16),
                vmem((MEMBERS, cap, part), BF16),
                vmem((MEMBERS, cap, part), BF16),
                vmem((rows, MEMBERS * cap), BF16),
                vmem((MEMBERS * cap, rows), BF16),
                vmem((CHIPS, 2, 2, half, part), BF16),
                vmem((rows, ff), F32),
                vmem((rows, ff), F32),
                vmem((rows, ff), BF16),
                vmem((strips, CHIPS, rows, LANES), F32),
                vmem((strips, CHIPS, rows, LANES), BF16),
                vmem((strips, CHIPS, rows, LANES), BF16),
                vmem((strips, 2, 2, half, LANES), BF16),
                vmem((strips, 2, 2, half, LANES), BF16),
                vmem((strips, 2, 2, 2, half, LANES), BF16),
                vmem((strips, 2, 2, 2, half, LANES), BF16),
                vmem((strips, 2, rows, LANES), BF16),
                vmem((strips, 2, rows, LANES), BF16),
                vmem((strips, MEMBERS, cap, LANES), BF16),
                vmem((strips, MEMBERS, cap, LANES), BF16),
                dma((19,)),
                dma((MEMBERS,)), dma((MEMBERS,)),
                dma((2, MEMBERS)), dma((2, MEMBERS)),
                dma((60,)), dma((CHIPS, 2, 2, 2)),
                dma((strips, CHIPS)), dma((strips, CHIPS)),
                dma((strips, 2, 2)), dma((strips, 2, 2)),
                dma((strips, 2, 2, 2)), dma((strips, 2, 2, 2)),
                dma((strips, 2)), dma((strips, 2)),
                dma((strips, MEMBERS)), dma((strips, MEMBERS)),
                dma((3,)), dma((3,)),
            ],
            compiler_params=pltpu.CompilerParams(
                collective_id=0, has_side_effects=True, vmem_limit_bytes=62 * 2**20
            ),
            name="routed_block",
        )(
            hidden_in,
            norm_gain,
            w_gate.reshape(CHIPS, 2, part, ff),
            w_up.reshape(CHIPS, 2, part, ff),
            w_down.reshape(ff, width),
            expert_ids.T,
            gate_weights.T,
        )

    return jax.shard_map(
        per_device,
        mesh=mesh,
        in_specs=(
            P(("pipe", "expert", "dp"), None),
            P("pipe", None),
            P("pipe", None, ("expert", "dp")),
            P("pipe", None, ("expert", "dp")),
            P("pipe", ("expert", "dp"), None),
            P(("pipe", "expert", "dp"), None),
            P(("pipe", "expert", "dp"), None),
        ),
        out_specs=P(("pipe", "expert", "dp"), None),
        check_vma=False,
    )
```

time: 318 us -> 105 us (0.33)
  waiting for transfers between devices: 253 us -> 0 us
  Pallas kernels: 0 us -> 102 us
  matrix products: 32.8 us -> 0 us
  between operations: 13.5 us -> 0.01 us
  other arithmetic: 9.89 us -> 0 us
  local copies, waits for them, and re-layouts: 6.12 us -> 2.69 us
    reduce_scatter x1 -> x0, waiting for transfers between devices: 141 us -> none  [per_device(): lax.psum_scatter(terms.astype(jnp.bfloat16), ('expert', 'dp'), scatter_di...]
    pallas_call x0 -> x1, Pallas kernels: none -> 102 us  [per_device(): pl.pallas_call(functools.partial(kernel, sections), out_shape=jax.ShapeDt...]
    all_gather x1 -> x0, waiting for transfers between devices: 75.7 us -> none  [per_device(): lax.all_gather(packed, ('expert', 'dp'), axis=0, tiled=True)]
    ppermute x1 -> x0, waiting for transfers between devices: 36.8 us -> none  [passed_along(): return lax.ppermute(block, axis, route)]
    dot_general x3 -> x0, matrix products: 32.8 us -> none  [the longest x1 12.4 us: expert_rows(): return jnp.dot(hidden, down_matrix, preferred_element_type=jnp.float32)]
    convert_element_type x4 -> x0, other arithmetic: 5.8 us -> none  [the longest x1 2.69 us: per_device(): (hidden_in.astype(jnp.float32) + own_weight[:, None] * branch).astype(jnp...]
    gather x2 -> x0, local copies, waits for them, and re-layouts: 4.19 us -> none  [the longest x1 3.18 us: per_device(): back = jnp.take(own_rows, jnp.clip(position, 0, capacity - 1), axis=0)]
  transfers between devices with their start and end apart: 3 -> 0, of which waited for: 3 -> 0; matrix products, arithmetic and copies ran while one was open for 0% -> 0% of each run, Pallas kernels for 0% -> 0%
where the time goes in v2:
time: 105 us; the launch traced here: 104 us
  Pallas kernels  102 us (97%)
  local copies, waits for them, and re-layouts  2.69 us (3%)
    pallas_call x1, Pallas kernels, per_device(): pl.pallas_call(functools.partial(kernel, sections), out_shape=jax.ShapeDt...  102 us
    unnamed x1, local copies, waits for them, and re-layouts  2.69 us

profile of v2, /device:TPU:1, one launch (start us, length us, event | category | flops | bytes accessed | tf_op | source)
XLA Modules:
  0.0 104.4 jit_solution(10897244813429396867)
XLA Ops:
  0.0 101.7 %routed_block.1 = bf16[128,6144]{1,0:T(8,128)(2,1)} custom-call(bf16[128,6144]{1,0:T(8,128)(2,1)} %x_hbm.1, f32[1,6144]{1,0:T(1,128)} %gain.1, bf16[8,2,384,512]{3,2,1,0:T(8,128)(2,1)} %bitcast.5, bf16[8,2,384,512]{3,2,1,0:T(8,128)(2,1)} %bitcast.6, bf16[512,6144]{1,0:T(8,128)(2,1)} %bitcast.7, s32[2,128]{1,0:T(2,128)} %bitcast.8, f32[2,128]{1,0:T(2,128)} %bitcast.9), custom_call_target="tpu_custom_call" | custom-call | tf_op jit(solution)/shard_map/routed_block/pallas_call | solution.py:514
  101.7 2.7 %copy.9 = bf16[128,6144]{1,0:T(8,128)(2,1)} copy(bf16[128,6144]{1,0:T(8,128)(2,1)} %routed_block.1) | data formatting | bytes 3145728

commit v3 on v2

v3 whole, which is shorter than its diff:
```python
import functools

import jax
import jax.numpy as jnp
from jax import lax
from jax.experimental import pallas as pl
from jax.experimental.pallas import tpu as pltpu
from jax.sharding import PartitionSpec as P

MESH = pl.DeviceIdType.MESH
F32 = jnp.float32
BF16 = jnp.bfloat16
CHIPS = 8
MEMBERS = 16
LANES = 128
TILE = 16


def iota(shape, dim):
    return lax.broadcasted_iota(jnp.int32, shape, dim).astype(F32)


def kernel(
    sections,
    x_hbm, gain_hbm, wg_hbm, wu_hbm, wd_hbm, ids_hbm, gw_hbm,
    out_hbm,
    x_v, x_in, out, gain, ids, gw, route, route_in, counts, counts_in, wg, wu, wd,
    packed_0, packed_1, slots_0, slots_1, pick, place, gath_0, gath_1, acc_g, acc_u, hid, own, core_out, core_in, opp_out, opp_in,
    near_out, near_in, sum_out, sum_in, back_out, back_in,
    load_sem, out_sem, a2a_s, a2a_r, gath_s, gath_r, pair_r, core_s, core_r,
    opp_s, opp_r, near_s, near_r, sum_s, sum_r, back_s, back_r, relay_s, relay_r,
):
    p, c, d = lax.axis_index("pipe"), lax.axis_index("expert"), lax.axis_index("dp")
    y, z = d // 4, d % 4
    me = d * 2 + c
    after, before = lax.rem(p + 1, sections), lax.rem(p + sections - 1, sections)
    tokens, width = x_v.shape
    packed, slots, gath = (packed_0, packed_1), (slots_0, slots_1), (gath_0, gath_1)
    cap = packed_1.shape[1]
    part = LANES + packed_1.shape[2]
    half = gath_0.shape[1]
    rows = 2 * half
    strips = part // LANES
    cuts = ((0, LANES), (LANES, part - LANES))

    def chip(other_y, step):
        yy = 1 - y if other_y else y
        return yy * 4 + (z + step) % 4

    up, down, across = chip(False, 1), chip(False, 3), chip(True, 0)
    to_up, to_down, to_across = (p, c, up), (p, c, down), (p, c, across)
    to_core = (p, 1 - c, d)

    def remote(src, dst, send, recv, device):
        return pltpu.make_async_remote_copy(
            src_ref=src, dst_ref=dst, send_sem=send, recv_sem=recv,
            device_id=device, device_id_type=MESH,
        )

    def loop(first, last, body):
        def step(k, carry):
            body(k)
            return carry

        lax.fori_loop(first, last, step, 0)

    def member(k):
        dd = (y + k // 8) % 2 * 4 + (z + k // 2) % 4
        e = (c + k) % 2
        return dd * 2 + e, (p, e, dd)

    load_x = pltpu.make_async_copy(x_hbm, x_v, load_sem.at[0])
    load_g = pltpu.make_async_copy(wg_hbm, wg, load_sem.at[1])
    load_u = pltpu.make_async_copy(wu_hbm, wu, load_sem.at[2])
    small = [
        pltpu.make_async_copy(src, dst, load_sem.at[4 + n])
        for n, (src, dst) in enumerate(((ids_hbm, ids), (gw_hbm, gw), (gain_hbm, gain)))
    ]
    small[0].start()
    small[1].start()
    load_x.start()
    small[2].start()

    barrier = pltpu.get_barrier_semaphore()

    def greet(device):
        pl.semaphore_signal(barrier, inc=1, device_id=device, device_id_type=MESH)

    loop(1, MEMBERS, lambda k: greet(member(k)[1]))
    greet((before, c, d))
    greet((before, c, across))

    small[0].wait()
    small[1].wait()
    square = (tokens, tokens)
    chosen = ids[...] == 0
    routed = jnp.max(jnp.where(chosen, 1.0, 0.0), axis=0, keepdims=True)
    weight = jnp.sum(jnp.where(chosen, gw[...], 0.0), axis=0, keepdims=True)
    routed_b = jnp.broadcast_to(routed, square)
    tri = jnp.where(iota(square, 0) <= iota(square, 1), 1.0, 0.0).astype(BF16)
    rank = jnp.dot(routed_b.astype(BF16), tri, preferred_element_type=F32)
    spot = jnp.where((routed_b > 0.5) & (rank - 1.0 == iota(square, 0)), 1.0, 0.0)
    spot_t = spot[:cap].astype(BF16)
    route[...] = jnp.where(
        iota(square, 1) < cap, spot.T, jnp.broadcast_to(weight, square).T
    )
    count = jnp.dot(
        routed_b[:TILE].astype(BF16), jnp.ones(square, BF16), preferred_element_type=F32
    ).astype(BF16)
    for i in range(MEMBERS):
        packed_0[i, cap:] = count

    load_x.wait()
    small[2].wait()
    load_g.start()
    load_u.start()
    for j in range(CHIPS):
        for e in range(2):
            pltpu.make_async_copy(
                wd_hbm.at[:, pl.ds((2 * j + e) * part, part)], wd.at[j, e], load_sem.at[3]
            ).start()

    def squares(j, total):
        for t in range(strips):
            at = pl.ds(pl.multiple_of(j * part + t * LANES, LANES), LANES)
            v = x_v[:, at].astype(F32)
            total = total + v * v
        return total

    total = lax.fori_loop(0, MEMBERS, squares, jnp.zeros((tokens, LANES), F32))
    scale = lax.rsqrt(jnp.sum(total, axis=1, keepdims=True) / width + 1e-05)

    def pack(j, q):
        start, size = cuts[q]
        for t in range(4):
            i = j * 4 + t
            at = pl.ds(pl.multiple_of(i * part + start, LANES), size)
            n = (x_v[:, at].astype(F32) * scale * gain[:, at]).astype(BF16)
            packed[q][i, :cap] = jnp.dot(
                spot_t, n, preferred_element_type=F32
            ).astype(BF16)

    loop(0, MEMBERS // 4, lambda j: pack(j, 0))
    pl.semaphore_wait(barrier, MEMBERS + 1)

    def slot_copy(k, q):
        i, device = member(k)
        return remote(
            packed[q].at[i], slots[q].at[me], a2a_s.at[q], a2a_r.at[q], device
        )

    def all_slot_copies(q):
        block = pl.ds(0, MEMBERS - 1)
        return remote(
            packed[q].at[block], slots[q].at[block], a2a_s.at[q], a2a_r.at[q], to_core
        )

    loop(1, MEMBERS, lambda k: slot_copy(MEMBERS - k, 0).start())
    loop(0, MEMBERS // 4, lambda j: pack(j, 1))
    loop(1, MEMBERS, lambda k: slot_copy(MEMBERS - k, 1).start())
    for q in range(2):
        slots[q][me] = packed[q][me]
    all_slot_copies(0).wait_recv()
    counts[...] = slots_0[:, cap:]
    counterpart = (after, c, d)
    relay_route = remote(route, route_in, relay_s.at[0], relay_r.at[0], counterpart)
    relay_route.start()
    relay_counts = remote(counts, counts_in, relay_s.at[1], relay_r.at[1], counterpart)
    relay_counts.start()

    off = jnp.zeros((1, LANES), F32)
    lane1 = iota((1, LANES), 1)
    high = lane1 - cap
    row_i = iota((rows, LANES), 0)
    for q in range(MEMBERS // 2):
        n0, n1 = counts[2 * q].astype(F32)[0:1], counts[2 * q + 1].astype(F32)[0:1]
        target = jnp.where(
            lane1 < cap,
            jnp.where(lane1 < n0, off + lane1, -1.0),
            jnp.where(high < n1, off + n0 + high, -1.0),
        )
        pick[:, q * LANES:(q + 1) * LANES] = jnp.where(row_i == target, 1.0, 0.0).astype(BF16)
        off = off + n0 + n1

    sends = [0, 0]

    def spot_of(j, e, h):
        return (j * 2 + e) * 2 + h

    def send_piece(j, h, q, device):
        ref = gath[q].at[spot_of(j, c, h)]
        if device is to_core:
            sem = pair_r.at[q, j]
        else:
            sem = gath_r.at[q, j, h]
        remote(ref, ref, gath_s.at[q], sem, device).start()
        sends[q] += 1

    def wait_piece(j, h, q):
        ref = gath[q].at[spot_of(j, c, h)]
        remote(ref, ref, gath_s.at[q], gath_r.at[q, j, h], to_core).wait_recv()

    def wait_pair(j, q):
        ref = gath[q].at[pl.ds(spot_of(j, 1 - c, 0), 2)]
        remote(ref, ref, gath_s.at[q], pair_r.at[q, j], to_core).wait_recv()

    def gather_sent(q):
        ref = gath[q].at[pl.ds(0, sends[q])]
        remote(ref, ref, gath_s.at[q], gath_r.at[q, 0, 0], to_core).wait_send()

    def multiply(j, q, first=False):
        start, size = cuts[q]
        wait_pair(j, q)

        def tile(n):
            at = pl.ds(pl.multiple_of(n * 256, 256), 256)
            cols = slice(start, start + size)
            a = jnp.concatenate(
                [
                    jnp.concatenate([gath[q][spot_of(j, e, h)] for e in range(2)], axis=1)
                    for h in range(2)
                ],
                axis=0,
            )
            for w, acc in ((wg, acc_g), (wu, acc_u)):
                b = jnp.concatenate([w[j, e, cols, at] for e in range(2)], axis=0)
                v = jnp.dot(a, b, preferred_element_type=F32)
                if first:
                    acc[:, at] = v
                else:
                    acc[:, at] += v

        loop(0, acc_g.shape[1] // 256, tile)

    def to_z(j, q, first):
        if first:
            send_piece(j, 0, q, to_up)
            send_piece(j, 1, q, to_down)
        else:
            send_piece(j, 1, q, to_up)
            send_piece(j, 0, q, to_down)

    def forward(below, above, q):
        wait_piece(below, 0, q)
        send_piece(below, 0, q, to_up)
        send_piece(below, 0, q, to_core)
        wait_piece(above, 1, q)
        send_piece(above, 1, q, to_down)
        send_piece(above, 1, q, to_core)

    def rest(below, above, q):
        wait_piece(below, 1, q)
        send_piece(below, 1, q, to_core)
        wait_piece(above, 0, q)
        send_piece(above, 0, q, to_core)

    def from_across(q):
        for h in range(2):
            wait_piece(across, h, q)
        to_z(across, q, True)
        to_z(across, q, False)
        for h in range(2):
            send_piece(across, h, q, to_core)

    def from_far(j, q):
        for h in range(2):
            wait_piece(j, h, q)
            send_piece(j, h, q, to_core)

    for q, (start, size) in enumerate(cuts):
        if q:
            all_slot_copies(q).wait_recv()
        all_slots = slots[q][:, :cap].reshape(MEMBERS * cap, size)
        for h in range(2):
            gath[q][spot_of(d, c, h)] = jnp.dot(
                pick[h * half:(h + 1) * half], all_slots, preferred_element_type=F32
            ).astype(BF16)
        to_z(d, q, True)
        send_piece(d, 0, q, to_across)
        send_piece(d, 1, q, to_across)
        to_z(d, q, False)
        send_piece(d, 0, q, to_core)
        send_piece(d, 1, q, to_core)

    aup, adown, far, afar = chip(True, 1), chip(True, 3), chip(False, 2), chip(True, 2)
    load_g.wait()
    load_u.wait()
    multiply(d, 0, first=True)
    forward(down, up, 0)
    from_across(0)
    rest(down, up, 0)

    relay_counts.wait_recv()
    off = jnp.zeros((1, LANES), F32)
    s_i, r_i = iota((cap, rows), 0), iota((cap, rows), 1)
    for i in range(MEMBERS):
        n = counts_in[i].astype(F32)[0:1]
        hit = (r_i - s_i == off[:, 0:1]) & (s_i < n[:, 0:1])
        place[i * cap:(i + 1) * cap] = jnp.where(hit, 1.0, 0.0).astype(BF16)
        off = off + n

    multiply(d, 1)
    multiply(across, 0)
    forward(down, up, 1)
    multiply(down, 0)
    multiply(up, 0)
    from_across(1)
    relay_x = remote(x_v, x_in, relay_s.at[2], relay_r.at[2], counterpart)
    relay_x.start()
    for q in range(2):
        all_slot_copies(q).wait_send()
    forward(adown, aup, 0)
    rest(adown, aup, 0)
    rest(down, up, 1)
    multiply(across, 1)
    multiply(adown, 0)
    multiply(aup, 0)
    multiply(down, 1)
    multiply(up, 1)
    from_far(far, 0)
    forward(adown, aup, 1)
    from_far(far, 1)
    multiply(far, 0)
    multiply(far, 1)
    rest(adown, aup, 1)
    from_far(afar, 0)
    multiply(adown, 1)
    from_far(afar, 1)
    multiply(afar, 0)
    multiply(aup, 1)
    multiply(afar, 1)

    def activate(n):
        at = pl.ds(pl.multiple_of(n * 128, 128), 128)
        g = acc_g[at]
        hid[at] = (g / (1.0 + jnp.exp(-g)) * acc_u[at]).astype(BF16)

    loop(0, rows // 128, activate)
    pltpu.make_async_copy(wd, wd, load_sem.at[3]).wait()

    order = [(o, s) for o in (True, False) for s in (2, 1, 3, 0)]
    core_copies = {}
    def project(q, k):
        j = chip(*order[k])
        cols = slice(q * LANES, (q + 1) * LANES)
        w = jnp.concatenate([wd[j, 1 - c, :, cols], wd[j, c, :, cols]], axis=1)
        v = jnp.dot(hid[...], w, preferred_element_type=F32)
        core_out[q, k] = v[:, :LANES].astype(BF16)
        cp = remote(
            core_out.at[q, k], core_in.at[q, k], core_s.at[0], core_r.at[q, k], to_core
        )
        cp.start()
        core_copies[q, k] = cp
        own[q, k] = v[:, LANES:]

    def both(q, k, h):
        at = pl.ds(h * half, half)
        return own[q, k, at] + core_in[q, k, at].astype(F32)

    def send_far(q, g):
        core_copies[q, 4 * g].wait_recv()
        for h, device in ((0, to_up), (1, to_down)):
            opp_out[q, g, h] = both(q, 4 * g, h).astype(BF16)
            remote(
                opp_out.at[q, g, h], opp_in.at[q, g, h], opp_s.at[0], opp_r.at[q, g, h], device
            ).start()

    def send_near(q, g, way, h, add):
        v = both(q, 4 * g + 1 + way, h)
        if add:
            v = v + opp_in[q, g, h].astype(F32)
        near_out[q, g, way, h] = v.astype(BF16)
        remote(
            near_out.at[q, g, way, h], near_in.at[q, g, way, h],
            near_s.at[0], near_r.at[q, g], to_down if way else to_up,
        ).start()

    def free_near(q, g):
        for way, h in ((0, 1), (1, 0)):
            core_copies[q, 4 * g + 1 + way].wait_recv()
            send_near(q, g, way, h, False)

    def independent(q):
        for g in range(2):
            send_far(q, g)
        for g in range(2):
            free_near(q, g)

    def dependent_group(q, g):
        for way, h in ((0, 0), (1, 1)):
            remote(
                opp_out.at[q, g, h], opp_in.at[q, g, h],
                opp_s.at[0], opp_r.at[q, g, h], to_up,
            ).wait_recv()
            send_near(q, g, way, h, True)

    def dependent(q):
        for g in range(2):
            dependent_group(q, g)

    def collect_group(q, g):
        core_copies[q, 4 * g + 3].wait_recv()
        remote(
            near_out.at[q, g], near_in.at[q, g], near_s.at[0], near_r.at[q, g], to_up
        ).wait_recv()
        for h in range(2):
            sum_out[q, g, h * half:(h + 1) * half] = (
                both(q, 4 * g + 3, h)
                + near_in[q, g, 0, h].astype(F32)
                + near_in[q, g, 1, h].astype(F32)
            ).astype(BF16)
        remote(
            sum_out.at[q, g], sum_in.at[q, y], sum_s.at[0], sum_r.at[q],
            (after, c, d if g else across),
        ).start()

    def collect(q):
        for g in range(2):
            collect_group(q, g)

    def back_copy(k, q):
        i, device = member(k)
        return remote(
            back_out.at[q, i], back_in.at[q, me], back_s.at[q], back_r.at[q], device
        )

    def all_back_copies(q):
        block = pl.ds(0, MEMBERS - 1)
        return remote(
            back_out.at[q, block], back_in.at[q, block], back_s.at[q], back_r.at[q], to_core
        )

    def unpack(q):
        remote(sum_out.at[q], sum_in.at[q], sum_s.at[0], sum_r.at[q], to_core).wait_recv()
        final = (sum_in[q, 0].astype(F32) + sum_in[q, 1].astype(F32)).astype(BF16)
        back_out[q] = (
            jnp.dot(place[...], final, preferred_element_type=F32)
            .astype(BF16)
            .reshape(MEMBERS, cap, LANES)
        )
        loop(1, MEMBERS, lambda k: back_copy(MEMBERS - k, q).start())
        back_in[q, me] = back_out[q, me]

    def finish(q):
        spread = route_in[:, :cap].astype(BF16)
        scale_in = route_in[:, cap:cap + 1]
        all_back_copies(q).wait_recv()

        for k in range(0, MEMBERS, 2):
            pair = jnp.concatenate([back_in[q, k], back_in[q, k + 1]], axis=1)
            term = scale_in * jnp.dot(spread, pair, preferred_element_type=F32)
            for t in range(2):
                start = (k + t) * part + q * LANES
                at = slice(start, start + LANES)
                v = x_in[:, at].astype(F32) + term[:, t * LANES:(t + 1) * LANES]
                out[:, at] = v.astype(BF16)
                pltpu.make_async_copy(out.at[:, at], out_hbm.at[:, at], out_sem.at[0]).start()

    def projects(q):
        for k in (0, 4, 1, 2, 5, 6, 3, 7):
            project(q, k)

    project(0, 0)
    project(0, 4)
    project(0, 1)
    send_far(0, 0)
    project(0, 2)
    send_far(0, 1)
    project(0, 5)
    project(0, 6)
    free_near(0, 0)
    project(0, 3)
    project(0, 7)
    free_near(0, 1)
    projects(1)
    dependent(0)
    independent(1)
    projects(2)
    collect(0)
    dependent(1)
    send_far(2, 0)
    free_near(2, 0)
    send_far(2, 1)
    collect(1)
    dependent_group(2, 0)
    free_near(2, 1)
    dependent_group(2, 1)
    collect(2)
    unpack(0)
    unpack(1)
    relay_route.wait_recv()
    relay_x.wait_recv()
    unpack(2)
    finish(0)
    finish(1)
    for q in range(2):
        gather_sent(q)
    for src, dst, sem in (
        (core_out, core_in, core_s), (opp_out, opp_in, opp_s),
        (near_out, near_in, near_s), (sum_out, sum_in, sum_s),
    ):
        remote(src, dst, sem.at[0], relay_r.at[0], to_core).wait_send()
    for cp in (relay_route, relay_counts, relay_x):
        cp.wait_send()
    for q in range(strips - 1):
        all_back_copies(q).wait_send()
    finish(2)
    all_back_copies(2).wait_send()
    pltpu.make_async_copy(out, out_hbm, out_sem.at[0]).wait()


def solution(mesh):
    sections = mesh.shape["pipe"]

    def per_device(hidden_in, norm_gain, w_gate, w_up, w_down, expert_ids, gate_weights):
        tokens, width = hidden_in.shape
        ff = w_gate.shape[2]
        cap = tokens // 2
        rows = MEMBERS * cap // 2
        half = rows // 2
        part = width // MEMBERS
        strips = part // LANES
        vmem = pltpu.VMEM
        dma = pltpu.SemaphoreType.DMA
        any_space = pl.BlockSpec(memory_space=pl.ANY)
        return pl.pallas_call(
            functools.partial(kernel, sections),
            out_shape=jax.ShapeDtypeStruct((tokens, width), BF16),
            in_specs=[any_space] * 7,
            out_specs=any_space,
            scratch_shapes=[
                vmem((tokens, width), BF16),
                vmem((tokens, width), BF16),
                vmem((tokens, width), BF16),
                vmem((1, width), F32),
                vmem((2, tokens), jnp.int32),
                vmem((2, tokens), F32),
                vmem((tokens, tokens), F32),
                vmem((tokens, tokens), F32),
                vmem((MEMBERS, TILE, LANES), BF16),
                vmem((MEMBERS, TILE, LANES), BF16),
                vmem((CHIPS, 2, part, ff), BF16),
                vmem((CHIPS, 2, part, ff), BF16),
                vmem((CHIPS, 2, ff, part), BF16),
                vmem((MEMBERS, cap + TILE, LANES), BF16),
                vmem((MEMBERS, cap, part - LANES), BF16),
                vmem((MEMBERS, cap + TILE, LANES), BF16),
                vmem((MEMBERS, cap, part - LANES), BF16),
                vmem((rows, MEMBERS * cap), BF16),
                vmem((MEMBERS * cap, rows), BF16),
                vmem((CHIPS * 4, half, LANES), BF16),
                vmem((CHIPS * 4, half, part - LANES), BF16),
                vmem((rows, ff), F32),
                vmem((rows, ff), F32),
                vmem((rows, ff), BF16),
                vmem((strips, CHIPS, rows, LANES), F32),
                vmem((strips, CHIPS, rows, LANES), BF16),
                vmem((strips, CHIPS, rows, LANES), BF16),
                vmem((strips, 2, 2, half, LANES), BF16),
                vmem((strips, 2, 2, half, LANES), BF16),
                vmem((strips, 2, 2, 2, half, LANES), BF16),
                vmem((strips, 2, 2, 2, half, LANES), BF16),
                vmem((strips, 2, rows, LANES), BF16),
                vmem((strips, 2, rows, LANES), BF16),
                vmem((strips, MEMBERS, cap, LANES), BF16),
                vmem((strips, MEMBERS, cap, LANES), BF16),
                dma((7,)), dma((1,)),
                dma((2,)), dma((2,)),
                dma((2,)), dma((2, CHIPS, 2)), dma((2, CHIPS)),
                dma((1,)), dma((strips, CHIPS)),
                dma((1,)), dma((strips, 2, 2)),
                dma((1,)), dma((strips, 2)),
                dma((1,)), dma((strips,)),
                dma((strips,)), dma((strips,)),
                dma((3,)), dma((3,)),
            ],
            compiler_params=pltpu.CompilerParams(
                collective_id=0, has_side_effects=True, vmem_limit_bytes=62 * 2**20
            ),
            name="routed_block",
        )(
            hidden_in,
            norm_gain,
            w_gate.reshape(CHIPS, 2, part, ff),
            w_up.reshape(CHIPS, 2, part, ff),
            w_down.reshape(ff, width),
            expert_ids.T,
            gate_weights.T,
        )

    return jax.shard_map(
        per_device,
        mesh=mesh,
        in_specs=(
            P(("pipe", "expert", "dp"), None),
            P("pipe", None),
            P("pipe", None, ("expert", "dp")),
            P("pipe", None, ("expert", "dp")),
            P("pipe", ("expert", "dp"), None),
            P(("pipe", "expert", "dp"), None),
            P(("pipe", "expert", "dp"), None),
        ),
        out_specs=P(("pipe", "expert", "dp"), None),
        check_vma=False,
    )
```

time: 105 us -> 96.9 us (0.923)
  Pallas kernels: 102 us -> 94.1 us
    pallas_call x1, Pallas kernels: 102 us -> 94.1 us  [per_device(): pl.pallas_call(functools.partial(kernel, sections), out_shape=jax.ShapeDt...]
where the time goes in v3:
time: 96.9 us; the launch traced here: 96.8 us
  Pallas kernels  94.1 us (97%)
  local copies, waits for them, and re-layouts  2.69 us (3%)
    pallas_call x1, Pallas kernels, per_device(): pl.pallas_call(functools.partial(kernel, sections), out_shape=jax.ShapeDt...  94.1 us
    unnamed x1, local copies, waits for them, and re-layouts  2.69 us

profile of v3, /device:TPU:1, one launch (start us, length us, event | category | flops | bytes accessed | tf_op | source)
XLA Modules:
  0.0 96.8 jit_solution(17005523273814664078)
XLA Ops:
  0.0 94.1 %routed_block.1 = bf16[128,6144]{1,0:T(8,128)(2,1)} custom-call(bf16[128,6144]{1,0:T(8,128)(2,1)} %x_hbm.1, f32[1,6144]{1,0:T(1,128)} %gain_hbm.1, bf16[8,2,384,512]{3,2,1,0:T(8,128)(2,1)} %bitcast.5, bf16[8,2,384,512]{3,2,1,0:T(8,128)(2,1)} %bitcast.6, bf16[512,6144]{1,0:T(8,128)(2,1)} %bitcast.7, s32[2,128]{1,0:T(2,128)} %bitcast.8, f32[2,128]{1,0:T(2,128)} %bitcast.9), custom_call_target="tpu_custom_call" | custom-call | tf_op jit(solution)/shard_map/routed_block/pallas_call | solution.py:526
  94.1 2.7 %copy.9 = bf16[128,6144]{1,0:T(8,128)(2,1)} copy(bf16[128,6144]{1,0:T(8,128)(2,1)} %routed_block.1) | data formatting | bytes 3145728

commit v4 on v3

--- a/solution.py
+++ b/solution.py
@@ -13,6 +13,7 @@
 CHIPS = 8
 MEMBERS = 16
 LANES = 128
+RELAY_PIECES = 4
 TILE = 16
 
 
@@ -24,11 +25,11 @@
     sections,
     x_hbm, gain_hbm, wg_hbm, wu_hbm, wd_hbm, ids_hbm, gw_hbm,
     out_hbm,
-    x_v, x_in, out, gain, ids, gw, route, route_in, counts, counts_in, wg, wu, wd,
+    x_v, x_mid, x_in, out, gain, ids, gw, route, route_in, counts, counts_in, wg, wu, wd,
     packed_0, packed_1, slots_0, slots_1, pick, place, gath_0, gath_1, acc_g, acc_u, hid, own, core_out, core_in, opp_out, opp_in,
     near_out, near_in, sum_out, sum_in, back_out, back_in,
     load_sem, out_sem, a2a_s, a2a_r, gath_s, gath_r, pair_r, core_s, core_r,
-    opp_s, opp_r, near_s, near_r, sum_s, sum_r, back_s, back_r, relay_s, relay_r,
+    opp_s, opp_r, near_s, near_r, sum_s, sum_r, back_s, back_r, relay_s, relay_r, mid_r,
 ):
     p, c, d = lax.axis_index("pipe"), lax.axis_index("expert"), lax.axis_index("dp")
     y, z = d // 4, d % 4
@@ -158,6 +159,20 @@
     loop(1, MEMBERS, lambda k: slot_copy(MEMBERS - k, 0).start())
     loop(0, MEMBERS // 4, lambda j: pack(j, 1))
     loop(1, MEMBERS, lambda k: slot_copy(MEMBERS - k, 1).start())
+
+    def relay_piece(i):
+        at = pl.ds(i * (tokens // RELAY_PIECES), tokens // RELAY_PIECES)
+        return remote(
+            x_v.at[at], x_mid.at[at], relay_s.at[2], mid_r.at[i], (after, c, across)
+        )
+
+    def relay_on(i):
+        relay_piece(i).wait_recv()
+        at = pl.ds(i * (tokens // RELAY_PIECES), tokens // RELAY_PIECES)
+        remote(x_mid.at[at], x_in.at[at], relay_s.at[3], relay_r.at[2], to_across).start()
+
+    for i in range(RELAY_PIECES):
+        relay_piece(i).start()
     for q in range(2):
         slots[q][me] = packed[q][me]
     all_slot_copies(0).wait_recv()
@@ -187,85 +202,36 @@
     def spot_of(j, e, h):
         return (j * 2 + e) * 2 + h
 
-    def send_piece(j, h, q, device):
+    def send_piece(j, h, q, *devices):
         ref = gath[q].at[spot_of(j, c, h)]
-        if device is to_core:
-            sem = pair_r.at[q, j]
-        else:
-            sem = gath_r.at[q, j, h]
-        remote(ref, ref, gath_s.at[q], sem, device).start()
-        sends[q] += 1
-
-    def wait_piece(j, h, q):
+        for device in devices:
+            sem = (pair_r if device is to_core else gath_r).at[q, j, h]
+            remote(ref, ref, gath_s.at[q], sem, device).start()
+            sends[q] += 1
+
+    def take_piece(j, h, q, *devices):
         ref = gath[q].at[spot_of(j, c, h)]
         remote(ref, ref, gath_s.at[q], gath_r.at[q, j, h], to_core).wait_recv()
-
-    def wait_pair(j, q):
-        ref = gath[q].at[pl.ds(spot_of(j, 1 - c, 0), 2)]
-        remote(ref, ref, gath_s.at[q], pair_r.at[q, j], to_core).wait_recv()
+        send_piece(j, h, q, *devices, to_core)
 
     def gather_sent(q):
         ref = gath[q].at[pl.ds(0, sends[q])]
         remote(ref, ref, gath_s.at[q], gath_r.at[q, 0, 0], to_core).wait_send()
 
-    def multiply(j, q, first=False):
+    def multiply(j, q, h, first=False):
+        other = gath[q].at[spot_of(j, 1 - c, h)]
+        remote(other, other, gath_s.at[q], pair_r.at[q, j, h], to_core).wait_recv()
         start, size = cuts[q]
-        wait_pair(j, q)
-
-        def tile(n):
-            at = pl.ds(pl.multiple_of(n * 256, 256), 256)
-            cols = slice(start, start + size)
-            a = jnp.concatenate(
-                [
-                    jnp.concatenate([gath[q][spot_of(j, e, h)] for e in range(2)], axis=1)
-                    for h in range(2)
-                ],
-                axis=0,
-            )
-            for w, acc in ((wg, acc_g), (wu, acc_u)):
-                b = jnp.concatenate([w[j, e, cols, at] for e in range(2)], axis=0)
-                v = jnp.dot(a, b, preferred_element_type=F32)
-                if first:
-                    acc[:, at] = v
-                else:
-                    acc[:, at] += v
-
-        loop(0, acc_g.shape[1] // 256, tile)
-
-    def to_z(j, q, first):
-        if first:
-            send_piece(j, 0, q, to_up)
-            send_piece(j, 1, q, to_down)
-        else:
-            send_piece(j, 1, q, to_up)
-            send_piece(j, 0, q, to_down)
-
-    def forward(below, above, q):
-        wait_piece(below, 0, q)
-        send_piece(below, 0, q, to_up)
-        send_piece(below, 0, q, to_core)
-        wait_piece(above, 1, q)
-        send_piece(above, 1, q, to_down)
-        send_piece(above, 1, q, to_core)
-
-    def rest(below, above, q):
-        wait_piece(below, 1, q)
-        send_piece(below, 1, q, to_core)
-        wait_piece(above, 0, q)
-        send_piece(above, 0, q, to_core)
-
-    def from_across(q):
-        for h in range(2):
-            wait_piece(across, h, q)
-        to_z(across, q, True)
-        to_z(across, q, False)
-        for h in range(2):
-            send_piece(across, h, q, to_core)
-
-    def from_far(j, q):
-        for h in range(2):
-            wait_piece(j, h, q)
-            send_piece(j, h, q, to_core)
+        cols = slice(start, start + size)
+        at = slice(h * half, (h + 1) * half)
+        a = jnp.concatenate([gath[q][spot_of(j, e, h)] for e in range(2)], axis=1)
+        for w, acc in ((wg, acc_g), (wu, acc_u)):
+            b = jnp.concatenate([w[j, e, cols] for e in range(2)], axis=0)
+            v = jnp.dot(a, b, preferred_element_type=F32)
+            if first:
+                acc[at] = v
+            else:
+                acc[at] += v
 
     for q, (start, size) in enumerate(cuts):
         if q:
@@ -275,148 +241,145 @@
             gath[q][spot_of(d, c, h)] = jnp.dot(
                 pick[h * half:(h + 1) * half], all_slots, preferred_element_type=F32
             ).astype(BF16)
-        to_z(d, q, True)
-        send_piece(d, 0, q, to_across)
-        send_piece(d, 1, q, to_across)
-        to_z(d, q, False)
-        send_piece(d, 0, q, to_core)
-        send_piece(d, 1, q, to_core)
+            if h == 0 or q == 0:
+                send_piece(d, h, q, to_up)
+            send_piece(d, h, q, to_down, to_across, to_core)
 
     aup, adown, far, afar = chip(True, 1), chip(True, 3), chip(False, 2), chip(True, 2)
     load_g.wait()
     load_u.wait()
-    multiply(d, 0, first=True)
-    forward(down, up, 0)
-    from_across(0)
-    rest(down, up, 0)
-
-    relay_counts.wait_recv()
-    off = jnp.zeros((1, LANES), F32)
-    s_i, r_i = iota((cap, rows), 0), iota((cap, rows), 1)
-    for i in range(MEMBERS):
-        n = counts_in[i].astype(F32)[0:1]
-        hit = (r_i - s_i == off[:, 0:1]) & (s_i < n[:, 0:1])
-        place[i * cap:(i + 1) * cap] = jnp.where(hit, 1.0, 0.0).astype(BF16)
-        off = off + n
-
-    multiply(d, 1)
-    multiply(across, 0)
-    forward(down, up, 1)
-    multiply(down, 0)
-    multiply(up, 0)
-    from_across(1)
-    relay_x = remote(x_v, x_in, relay_s.at[2], relay_r.at[2], counterpart)
-    relay_x.start()
+    multiply(d, 0, 0, first=True)
+    multiply(d, 0, 1, first=True)
+    take_piece(down, 0, 0, to_up)
+    take_piece(up, 1, 0, to_down)
+    take_piece(up, 0, 0)
+    take_piece(down, 1, 0)
+    multiply(d, 1, 0)
+    multiply(d, 1, 1)
+    take_piece(across, 0, 0, to_up, to_down)
+    take_piece(across, 1, 0, to_down)
+    multiply(down, 0, 0)
+    multiply(up, 0, 0)
+    take_piece(across, 0, 1, to_up, to_down)
+    take_piece(down, 0, 1, to_up)
+    take_piece(up, 0, 1)
+    multiply(across, 0, 0)
+    multiply(across, 0, 1)
+    multiply(down, 0, 1)
+    multiply(up, 0, 1)
+    take_piece(across, 1, 1, to_down)
+    relay_on(0)
+    relay_on(1)
     for q in range(2):
         all_slot_copies(q).wait_send()
-    forward(adown, aup, 0)
-    rest(adown, aup, 0)
-    rest(down, up, 1)
-    multiply(across, 1)
-    multiply(adown, 0)
-    multiply(aup, 0)
-    multiply(down, 1)
-    multiply(up, 1)
-    from_far(far, 0)
-    forward(adown, aup, 1)
-    from_far(far, 1)
-    multiply(far, 0)
-    multiply(far, 1)
-    rest(adown, aup, 1)
-    from_far(afar, 0)
-    multiply(adown, 1)
-    from_far(afar, 1)
-    multiply(afar, 0)
-    multiply(aup, 1)
-    multiply(afar, 1)
-
-    def activate(n):
-        at = pl.ds(pl.multiple_of(n * 128, 128), 128)
-        g = acc_g[at]
-        hid[at] = (g / (1.0 + jnp.exp(-g)) * acc_u[at]).astype(BF16)
-
-    loop(0, rows // 128, activate)
-    pltpu.make_async_copy(wd, wd, load_sem.at[3]).wait()
-
-    order = [(o, s) for o in (True, False) for s in (2, 1, 3, 0)]
-    core_copies = {}
-    def project(q, k):
-        j = chip(*order[k])
+    take_piece(adown, 0, 0, to_up)
+    take_piece(up, 1, 1, to_down)
+    take_piece(far, 0, 0)
+    multiply(across, 1, 0)
+    multiply(down, 1, 0)
+    multiply(up, 1, 0)
+    multiply(far, 0, 0)
+
+    take_piece(aup, 0, 0)
+    take_piece(adown, 0, 1, to_up)
+    send_piece(d, 1, 1, to_up)
+    send_piece(across, 1, 0, to_up)
+    send_piece(across, 1, 1, to_up)
+    multiply(up, 1, 1)
+    take_piece(aup, 1, 0, to_down)
+    take_piece(far, 1, 0)
+    multiply(across, 1, 1)
+    multiply(adown, 0, 0)
+    multiply(aup, 0, 0)
+    multiply(adown, 1, 0)
+    multiply(far, 0, 1)
+    multiply(aup, 0, 1)
+    take_piece(far, 0, 1)
+    take_piece(aup, 0, 1)
+    take_piece(afar, 0, 0)
+    multiply(far, 1, 0)
+    multiply(aup, 1, 0)
+    take_piece(aup, 1, 1, to_down)
+    relay_on(2)
+    multiply(afar, 0, 0)
+    take_piece(afar, 0, 1)
+    multiply(aup, 1, 1)
+    multiply(afar, 1, 0)
+
+    def activate(h):
+        def block(n):
+            at = pl.ds(pl.multiple_of(h * half + n * 128, 128), 128)
+            g = acc_g[at]
+            hid[at] = (g / (1.0 + jnp.exp(-g)) * acc_u[at]).astype(BF16)
+
+        loop(0, half // 128, block)
+
+    FAR, UP, DOWN, HERE = range(4)
+    steps = (2, 1, 3, 0)
+
+    def core_copy(q, h, t):
+        return remote(
+            core_out.at[q, h, t], core_in.at[q, h, t], core_s.at[0], core_r.at[q, h, t], to_core
+        )
+
+    def project(q, h, *targets):
         cols = slice(q * LANES, (q + 1) * LANES)
-        w = jnp.concatenate([wd[j, 1 - c, :, cols], wd[j, c, :, cols]], axis=1)
-        v = jnp.dot(hid[...], w, preferred_element_type=F32)
-        core_out[q, k] = v[:, :LANES].astype(BF16)
-        cp = remote(
-            core_out.at[q, k], core_in.at[q, k], core_s.at[0], core_r.at[q, k], to_core
-        )
-        cp.start()
-        core_copies[q, k] = cp
-        own[q, k] = v[:, LANES:]
-
-    def both(q, k, h):
-        at = pl.ds(h * half, half)
-        return own[q, k, at] + core_in[q, k, at].astype(F32)
-
-    def send_far(q, g):
-        core_copies[q, 4 * g].wait_recv()
-        for h, device in ((0, to_up), (1, to_down)):
-            opp_out[q, g, h] = both(q, 4 * g, h).astype(BF16)
+        for t in targets:
+            chips = (chip(True, steps[t]), chip(False, steps[t]))
+            w = jnp.concatenate(
+                [wd[j, e, :, cols] for j in chips for e in (1 - c, c)], axis=1
+            )
+            v = jnp.dot(hid[h * half:(h + 1) * half], w, preferred_element_type=F32)
+            for g in range(2):
+                core_out[q, h, t, g] = v[:, 2 * g * LANES:(2 * g + 1) * LANES].astype(BF16)
+                own[q, h, t, g] = v[:, (2 * g + 1) * LANES:(2 * g + 2) * LANES]
+            core_copy(q, h, t).start()
+
+    def both(q, h, t):
+        return own[q, h, t] + core_in[q, h, t].astype(F32)
+
+    def far_copy(q, h):
+        return remote(
+            opp_out.at[q, h], opp_in.at[q, h], opp_s.at[0], opp_r.at[q, h],
+            to_down if h else to_up,
+        )
+
+    def send_far(q, h):
+        core_copy(q, h, FAR).wait_recv()
+        opp_out[q, h] = both(q, h, FAR).astype(BF16)
+        far_copy(q, h).start()
+
+    def send_near(q, h, way, v):
+        near_out[q, h, way] = v.astype(BF16)
+        remote(
+            near_out.at[q, h, way], near_in.at[q, h, way], near_s.at[0], near_r.at[q, h],
+            to_down if way else to_up,
+        ).start()
+
+    def send_free(q, h):
+        t = UP if h else DOWN
+        core_copy(q, h, t).wait_recv()
+        send_near(q, h, 1 - h, both(q, h, t))
+
+    def send_joined(q, h):
+        t = DOWN if h else UP
+        core_copy(q, h, t).wait_recv()
+        far_copy(q, h).wait_recv()
+        send_near(q, h, h, both(q, h, t) + opp_in[q, h].astype(F32))
+
+    def collect(q, h):
+        core_copy(q, h, HERE).wait_recv()
+        remote(
+            near_out.at[q, h], near_in.at[q, h], near_s.at[0], near_r.at[q, h], to_up
+        ).wait_recv()
+        sum_out[q, h] = (
+            both(q, h, HERE) + near_in[q, h, 0].astype(F32) + near_in[q, h, 1].astype(F32)
+        ).astype(BF16)
+        for g in range(2):
             remote(
-                opp_out.at[q, g, h], opp_in.at[q, g, h], opp_s.at[0], opp_r.at[q, g, h], device
+                sum_out.at[q, h, g], sum_in.at[q, y, h], sum_s.at[0], sum_r.at[q],
+                (after, c, d if g else across),
             ).start()
-
-    def send_near(q, g, way, h, add):
-        v = both(q, 4 * g + 1 + way, h)
-        if add:
-            v = v + opp_in[q, g, h].astype(F32)
-        near_out[q, g, way, h] = v.astype(BF16)
-        remote(
-            near_out.at[q, g, way, h], near_in.at[q, g, way, h],
-            near_s.at[0], near_r.at[q, g], to_down if way else to_up,
-        ).start()
-
-    def free_near(q, g):
-        for way, h in ((0, 1), (1, 0)):
-            core_copies[q, 4 * g + 1 + way].wait_recv()
-            send_near(q, g, way, h, False)
-
-    def independent(q):
-        for g in range(2):
-            send_far(q, g)
-        for g in range(2):
-            free_near(q, g)
-
-    def dependent_group(q, g):
-        for way, h in ((0, 0), (1, 1)):
-            remote(
-                opp_out.at[q, g, h], opp_in.at[q, g, h],
-                opp_s.at[0], opp_r.at[q, g, h], to_up,
-            ).wait_recv()
-            send_near(q, g, way, h, True)
-
-    def dependent(q):
-        for g in range(2):
-            dependent_group(q, g)
-
-    def collect_group(q, g):
-        core_copies[q, 4 * g + 3].wait_recv()
-        remote(
-            near_out.at[q, g], near_in.at[q, g], near_s.at[0], near_r.at[q, g], to_up
-        ).wait_recv()
-        for h in range(2):
-            sum_out[q, g, h * half:(h + 1) * half] = (
-                both(q, 4 * g + 3, h)
-                + near_in[q, g, 0, h].astype(F32)
-                + near_in[q, g, 1, h].astype(F32)
-            ).astype(BF16)
-        remote(
-            sum_out.at[q, g], sum_in.at[q, y], sum_s.at[0], sum_r.at[q],
-            (after, c, d if g else across),
-        ).start()
-
-    def collect(q):
-        for g in range(2):
-            collect_group(q, g)
 
     def back_copy(k, q):
         i, device = member(k)
@@ -433,6 +396,7 @@
     def unpack(q):
         remote(sum_out.at[q], sum_in.at[q], sum_s.at[0], sum_r.at[q], to_core).wait_recv()
         final = (sum_in[q, 0].astype(F32) + sum_in[q, 1].astype(F32)).astype(BF16)
+        final = final.reshape(rows, LANES)
         back_out[q] = (
             jnp.dot(place[...], final, preferred_element_type=F32)
             .astype(BF16)
@@ -456,39 +420,74 @@
                 out[:, at] = v.astype(BF16)
                 pltpu.make_async_copy(out.at[:, at], out_hbm.at[:, at], out_sem.at[0]).start()
 
-    def projects(q):
-        for k in (0, 4, 1, 2, 5, 6, 3, 7):
-            project(q, k)
-
-    project(0, 0)
-    project(0, 4)
-    project(0, 1)
+    activate(0)
+    pltpu.make_async_copy(wd, wd, load_sem.at[3]).wait()
+    project(0, 0, FAR, DOWN, UP)
+    take_piece(far, 1, 1)
+    take_piece(down, 1, 1)
     send_far(0, 0)
-    project(0, 2)
+    send_free(0, 0)
+    project(0, 0, HERE)
+    project(1, 0, FAR, DOWN, UP)
+    take_piece(afar, 1, 0)
+    take_piece(adown, 1, 0)
+    multiply(far, 1, 1)
+    send_far(1, 0)
+    send_free(1, 0)
+    multiply(down, 1, 1)
+    multiply(afar, 0, 1)
+    multiply(adown, 0, 1)
+    project(1, 0, HERE)
+    project(2, 0, FAR, DOWN, UP)
+    relay_on(3)
+    take_piece(afar, 1, 1)
+    take_piece(adown, 1, 1)
+    send_far(2, 0)
+    send_free(2, 0)
+    project(2, 0, HERE)
+    multiply(afar, 1, 1)
+    multiply(adown, 1, 1)
+    activate(1)
+    send_joined(0, 0)
+    project(0, 1, FAR, UP, DOWN)
     send_far(0, 1)
-    project(0, 5)
-    project(0, 6)
-    free_near(0, 0)
-    project(0, 3)
-    project(0, 7)
-    free_near(0, 1)
-    projects(1)
-    dependent(0)
-    independent(1)
-    projects(2)
-    collect(0)
-    dependent(1)
-    send_far(2, 0)
-    free_near(2, 0)
+    project(0, 1, HERE)
+    project(1, 1, FAR)
+    send_joined(1, 0)
+    send_free(0, 1)
+    project(1, 1, UP, DOWN)
+    send_far(1, 1)
+    project(1, 1, HERE)
+    project(2, 1, FAR)
+    send_joined(2, 0)
+    send_free(1, 1)
+    project(2, 1, UP, DOWN)
     send_far(2, 1)
-    collect(1)
-    dependent_group(2, 0)
-    free_near(2, 1)
-    dependent_group(2, 1)
-    collect(2)
+    send_free(2, 1)
+    project(2, 1, HERE)
+
+    relay_counts.wait_recv()
+    off = jnp.zeros((1, LANES), F32)
+    s_i, r_i = iota((cap, rows), 0), iota((cap, rows), 1)
+    for i in range(MEMBERS):
+        n = counts_in[i].astype(F32)[0:1]
+        hit = (r_i - s_i == off[:, 0:1]) & (s_i < n[:, 0:1])
+        place[i * cap:(i + 1) * cap] = jnp.where(hit, 1.0, 0.0).astype(BF16)
+        off = off + n
+
+    collect(0, 0)
+    send_joined(0, 1)
+    collect(1, 0)
+    send_joined(1, 1)
+    send_joined(2, 1)
+    collect(2, 0)
+    collect(0, 1)
+    collect(1, 1)
+    collect(2, 1)
     unpack(0)
     unpack(1)
     relay_route.wait_recv()
+    relay_x = remote(x_mid, x_in, relay_s.at[3], relay_r.at[2], to_across)
     relay_x.wait_recv()
     unpack(2)
     finish(0)
@@ -500,7 +499,8 @@
         (near_out, near_in, near_s), (sum_out, sum_in, sum_s),
     ):
         remote(src, dst, sem.at[0], relay_r.at[0], to_core).wait_send()
-    for cp in (relay_route, relay_counts, relay_x):
+    relay_first = remote(x_v, x_mid, relay_s.at[2], mid_r.at[0], to_across)
+    for cp in (relay_route, relay_counts, relay_first, relay_x):
         cp.wait_send()
     for q in range(strips - 1):
         all_back_copies(q).wait_send()
@@ -529,6 +529,7 @@
             in_specs=[any_space] * 7,
             out_specs=any_space,
             scratch_shapes=[
+                vmem((tokens, width), BF16),
                 vmem((tokens, width), BF16),
                 vmem((tokens, width), BF16),
                 vmem((tokens, width), BF16),
@@ -553,26 +554,26 @@
                 vmem((rows, ff), F32),
                 vmem((rows, ff), F32),
                 vmem((rows, ff), BF16),
-                vmem((strips, CHIPS, rows, LANES), F32),
-                vmem((strips, CHIPS, rows, LANES), BF16),
-                vmem((strips, CHIPS, rows, LANES), BF16),
+                vmem((strips, 2, 4, 2, half, LANES), F32),
+                vmem((strips, 2, 4, 2, half, LANES), BF16),
+                vmem((strips, 2, 4, 2, half, LANES), BF16),
                 vmem((strips, 2, 2, half, LANES), BF16),
                 vmem((strips, 2, 2, half, LANES), BF16),
                 vmem((strips, 2, 2, 2, half, LANES), BF16),
                 vmem((strips, 2, 2, 2, half, LANES), BF16),
-                vmem((strips, 2, rows, LANES), BF16),
-                vmem((strips, 2, rows, LANES), BF16),
+                vmem((strips, 2, 2, half, LANES), BF16),
+                vmem((strips, 2, 2, half, LANES), BF16),
                 vmem((strips, MEMBERS, cap, LANES), BF16),
                 vmem((strips, MEMBERS, cap, LANES), BF16),
                 dma((7,)), dma((1,)),
                 dma((2,)), dma((2,)),
-                dma((2,)), dma((2, CHIPS, 2)), dma((2, CHIPS)),
-                dma((1,)), dma((strips, CHIPS)),
-                dma((1,)), dma((strips, 2, 2)),
+                dma((2,)), dma((2, CHIPS, 2)), dma((2, CHIPS, 2)),
+                dma((1,)), dma((strips, 2, 4)),
+                dma((1,)), dma((strips, 2)),
                 dma((1,)), dma((strips, 2)),
                 dma((1,)), dma((strips,)),
                 dma((strips,)), dma((strips,)),
-                dma((3,)), dma((3,)),
+                dma((4,)), dma((3,)), dma((RELAY_PIECES,)),
             ],
             compiler_params=pltpu.CompilerParams(
                 collective_id=0, has_side_effects=True, vmem_limit_bytes=62 * 2**20

time: 96.9 us -> 91.4 us (0.943)
  Pallas kernels: 94.1 us -> 88.5 us
    pallas_call x1, Pallas kernels: 94.1 us -> 88.5 us  [per_device(): pl.pallas_call(functools.partial(kernel, sections), out_shape=jax.ShapeDt...]
where the time goes in v4:
time: 91.4 us; the launch traced here: 91.2 us
  Pallas kernels  88.5 us (97%)
  local copies, waits for them, and re-layouts  2.69 us (3%)
    pallas_call x1, Pallas kernels, per_device(): pl.pallas_call(functools.partial(kernel, sections), out_shape=jax.ShapeDt...  88.5 us
    unnamed x1, local copies, waits for them, and re-layouts  2.69 us

profile of v4, /device:TPU:1, one launch (start us, length us, event | category | flops | bytes accessed | tf_op | source)
XLA Modules:
  0.0 91.2 jit_solution(10099709014229906654)
XLA Ops:
  0.0 88.5 %routed_block.1 = bf16[128,6144]{1,0:T(8,128)(2,1)} custom-call(bf16[128,6144]{1,0:T(8,128)(2,1)} %x_hbm.1, f32[1,6144]{1,0:T(1,128)} %gain_hbm.1, bf16[8,2,384,512]{3,2,1,0:T(8,128)(2,1)} %bitcast.5, bf16[8,2,384,512]{3,2,1,0:T(8,128)(2,1)} %bitcast.6, bf16[512,6144]{1,0:T(8,128)(2,1)} %bitcast.7, s32[2,128]{1,0:T(2,128)} %bitcast.8, f32[2,128]{1,0:T(2,128)} %bitcast.9), custom_call_target="tpu_custom_call" | custom-call | tf_op jit(solution)/shard_map/routed_block/pallas_call | solution.py:526
  88.6 2.7 %copy.9 = bf16[128,6144]{1,0:T(8,128)(2,1)} copy(bf16[128,6144]{1,0:T(8,128)(2,1)} %routed_block.1) | data formatting | bytes 3145728

commit v5 on v4

--- a/solution.py
+++ b/solution.py
@@ -14,6 +14,8 @@
 MEMBERS = 16
 LANES = 128
 RELAY_PIECES = 4
+X_LOADS = 4
+FINISH_STEPS = 4
 TILE = 16
 
 
@@ -24,10 +26,10 @@
 def kernel(
     sections,
     x_hbm, gain_hbm, wg_hbm, wu_hbm, wd_hbm, ids_hbm, gw_hbm,
-    out_hbm,
-    x_v, x_mid, x_in, out, gain, ids, gw, route, route_in, counts, counts_in, wg, wu, wd,
+    x_in, back_in, route_in,
+    x_v, x_mid, gain, ids, gw, route, counts, counts_in, wg, wu, wd,
     packed_0, packed_1, slots_0, slots_1, pick, place, gath_0, gath_1, acc_g, acc_u, hid, own, core_out, core_in, opp_out, opp_in,
-    near_out, near_in, sum_out, sum_in, back_out, back_in,
+    near_out, near_in, sum_out, sum_in, partial, back_out,
     load_sem, out_sem, a2a_s, a2a_r, gath_s, gath_r, pair_r, core_s, core_r,
     opp_s, opp_r, near_s, near_r, sum_s, sum_r, back_s, back_r, relay_s, relay_r, mid_r,
 ):
@@ -70,16 +72,24 @@
         e = (c + k) % 2
         return dd * 2 + e, (p, e, dd)
 
-    load_x = pltpu.make_async_copy(x_hbm, x_v, load_sem.at[0])
-    load_g = pltpu.make_async_copy(wg_hbm, wg, load_sem.at[1])
-    load_u = pltpu.make_async_copy(wu_hbm, wu, load_sem.at[2])
+    block = width // X_LOADS
+    loads_x = [
+        pltpu.make_async_copy(
+            x_hbm.at[:, pl.ds(n * block, block)], x_v.at[:, pl.ds(n * block, block)],
+            load_sem.at[6 + n],
+        )
+        for n in range(X_LOADS)
+    ]
+    load_g = pltpu.make_async_copy(wg_hbm, wg, load_sem.at[0])
+    load_u = pltpu.make_async_copy(wu_hbm, wu, load_sem.at[1])
     small = [
-        pltpu.make_async_copy(src, dst, load_sem.at[4 + n])
+        pltpu.make_async_copy(src, dst, load_sem.at[3 + n])
         for n, (src, dst) in enumerate(((ids_hbm, ids), (gw_hbm, gw), (gain_hbm, gain)))
     ]
     small[0].start()
     small[1].start()
-    load_x.start()
+    for cp in loads_x:
+        cp.start()
     small[2].start()
 
     barrier = pltpu.get_barrier_semaphore()
@@ -111,25 +121,22 @@
     for i in range(MEMBERS):
         packed_0[i, cap:] = count
 
-    load_x.wait()
+    total = jnp.zeros((tokens, LANES), F32)
+    for n, cp in enumerate(loads_x):
+        cp.wait()
+        for t in range(block // LANES):
+            start = n * block + t * LANES
+            v = x_v[:, start:start + LANES].astype(F32)
+            total = total + v * v
+    scale = lax.rsqrt(jnp.sum(total, axis=1, keepdims=True) / width + 1e-05)
     small[2].wait()
     load_g.start()
     load_u.start()
     for j in range(CHIPS):
         for e in range(2):
             pltpu.make_async_copy(
-                wd_hbm.at[:, pl.ds((2 * j + e) * part, part)], wd.at[j, e], load_sem.at[3]
+                wd_hbm.at[:, pl.ds((2 * j + e) * part, part)], wd.at[j, e], load_sem.at[2]
             ).start()
-
-    def squares(j, total):
-        for t in range(strips):
-            at = pl.ds(pl.multiple_of(j * part + t * LANES, LANES), LANES)
-            v = x_v[:, at].astype(F32)
-            total = total + v * v
-        return total
-
-    total = lax.fori_loop(0, MEMBERS, squares, jnp.zeros((tokens, LANES), F32))
-    scale = lax.rsqrt(jnp.sum(total, axis=1, keepdims=True) / width + 1e-05)
 
     def pack(j, q):
         start, size = cuts[q]
@@ -156,9 +163,11 @@
             packed[q].at[block], slots[q].at[block], a2a_s.at[q], a2a_r.at[q], to_core
         )
 
-    loop(1, MEMBERS, lambda k: slot_copy(MEMBERS - k, 0).start())
+    for k in range(MEMBERS - 1, 0, -1):
+        slot_copy(k, 0).start()
     loop(0, MEMBERS // 4, lambda j: pack(j, 1))
-    loop(1, MEMBERS, lambda k: slot_copy(MEMBERS - k, 1).start())
+    for k in range(MEMBERS - 1, 0, -1):
+        slot_copy(k, 1).start()
 
     def relay_piece(i):
         at = pl.ds(i * (tokens // RELAY_PIECES), tokens // RELAY_PIECES)
@@ -269,7 +278,6 @@
     multiply(up, 0, 1)
     take_piece(across, 1, 1, to_down)
     relay_on(0)
-    relay_on(1)
     for q in range(2):
         all_slot_copies(q).wait_send()
     take_piece(adown, 0, 0, to_up)
@@ -280,6 +288,7 @@
     multiply(up, 1, 0)
     multiply(far, 0, 0)
 
+    relay_on(1)
     take_piece(aup, 0, 0)
     take_piece(adown, 0, 1, to_up)
     send_piece(d, 1, 1, to_up)
@@ -349,12 +358,27 @@
         opp_out[q, h] = both(q, h, FAR).astype(BF16)
         far_copy(q, h).start()
 
+    last = (strips - 1, 1)
+
+    def near_copies(q, h, way):
+        device = to_down if way else to_up
+        if (q, h) != last:
+            return [remote(
+                near_out.at[q, h, way], near_in.at[q, h, way],
+                near_s.at[0], near_r.at[q, h, 0], device,
+            )]
+        return [
+            remote(
+                near_out.at[q, h, way, g], near_in.at[q, h, way, g],
+                near_s.at[0], near_r.at[q, h, g], device,
+            )
+            for g in (1, 0)
+        ]
+
     def send_near(q, h, way, v):
         near_out[q, h, way] = v.astype(BF16)
-        remote(
-            near_out.at[q, h, way], near_in.at[q, h, way], near_s.at[0], near_r.at[q, h],
-            to_down if way else to_up,
-        ).start()
+        for cp in near_copies(q, h, way):
+            cp.start()
 
     def send_free(q, h):
         t = UP if h else DOWN
@@ -367,19 +391,34 @@
         far_copy(q, h).wait_recv()
         send_near(q, h, h, both(q, h, t) + opp_in[q, h].astype(F32))
 
+    def send_sum(q, h, g):
+        remote(
+            sum_out.at[q, h, g], sum_in.at[q, h, y], sum_s.at[0], sum_r.at[q, h],
+            (after, c, d if g else across),
+        ).start()
+
     def collect(q, h):
         core_copy(q, h, HERE).wait_recv()
-        remote(
-            near_out.at[q, h], near_in.at[q, h], near_s.at[0], near_r.at[q, h], to_up
-        ).wait_recv()
-        sum_out[q, h] = (
-            both(q, h, HERE) + near_in[q, h, 0].astype(F32) + near_in[q, h, 1].astype(F32)
-        ).astype(BF16)
-        for g in range(2):
+        if (q, h) != last:
             remote(
-                sum_out.at[q, h, g], sum_in.at[q, y, h], sum_s.at[0], sum_r.at[q],
-                (after, c, d if g else across),
-            ).start()
+                near_out.at[q, h], near_in.at[q, h], near_s.at[0], near_r.at[q, h, 0], to_up
+            ).wait_recv()
+            sum_out[q, h] = (
+                both(q, h, HERE) + near_in[q, h, 0].astype(F32) + near_in[q, h, 1].astype(F32)
+            ).astype(BF16)
+            send_sum(q, h, 1)
+            send_sum(q, h, 0)
+            return
+        for g in (1, 0):
+            remote(
+                near_out.at[q, h, :, g], near_in.at[q, h, :, g],
+                near_s.at[0], near_r.at[q, h, g], to_up,
+            ).wait_recv()
+            sum_out[q, h, g] = (
+                own[q, h, HERE, g] + core_in[q, h, HERE, g].astype(F32)
+                + near_in[q, h, 0, g].astype(F32) + near_in[q, h, 1, g].astype(F32)
+            ).astype(BF16)
+            send_sum(q, h, g)
 
     def back_copy(k, q):
         i, device = member(k)
@@ -393,35 +432,41 @@
             back_out.at[q, block], back_in.at[q, block], back_s.at[q], back_r.at[q], to_core
         )
 
+    sides = ((1 - y, CHIPS), (y, 0))
+
+    def spread_rows(q, h, yy):
+        final = (sum_in[q, h, 0].astype(F32) + sum_in[q, h, 1].astype(F32)).astype(BF16)
+        at = pl.ds(pl.multiple_of(yy * (CHIPS * cap), CHIPS * cap), CHIPS * cap)
+        return jnp.dot(
+            place[at, h * half:(h + 1) * half], final, preferred_element_type=F32
+        )
+
+    def wait_sums(q, h):
+        ref = sum_in.at[q, h]
+        remote(ref, ref, sum_s.at[0], sum_r.at[q, h], to_core).wait_recv()
+
+    def unpack_first(q):
+        wait_sums(q, 0)
+        for t, (yy, first) in enumerate(sides):
+            partial[q % 2, t] = spread_rows(q, 0, yy)
+
     def unpack(q):
-        remote(sum_out.at[q], sum_in.at[q], sum_s.at[0], sum_r.at[q], to_core).wait_recv()
-        final = (sum_in[q, 0].astype(F32) + sum_in[q, 1].astype(F32)).astype(BF16)
-        final = final.reshape(rows, LANES)
-        back_out[q] = (
-            jnp.dot(place[...], final, preferred_element_type=F32)
-            .astype(BF16)
-            .reshape(MEMBERS, cap, LANES)
-        )
-        loop(1, MEMBERS, lambda k: back_copy(MEMBERS - k, q).start())
-        back_in[q, me] = back_out[q, me]
-
-    def finish(q):
-        spread = route_in[:, :cap].astype(BF16)
-        scale_in = route_in[:, cap:cap + 1]
-        all_back_copies(q).wait_recv()
-
-        for k in range(0, MEMBERS, 2):
-            pair = jnp.concatenate([back_in[q, k], back_in[q, k + 1]], axis=1)
-            term = scale_in * jnp.dot(spread, pair, preferred_element_type=F32)
-            for t in range(2):
-                start = (k + t) * part + q * LANES
-                at = slice(start, start + LANES)
-                v = x_in[:, at].astype(F32) + term[:, t * LANES:(t + 1) * LANES]
-                out[:, at] = v.astype(BF16)
-                pltpu.make_async_copy(out.at[:, at], out_hbm.at[:, at], out_sem.at[0]).start()
+        wait_sums(q, 1)
+        for t, (yy, first) in enumerate(sides):
+            back_out[q, pl.ds(yy * CHIPS, CHIPS)] = (
+                (partial[q % 2, t] + spread_rows(q, 1, yy))
+                .astype(BF16)
+                .reshape(CHIPS, cap, LANES)
+            )
+            for k in range(first + CHIPS - 1, max(first, 1) - 1, -1):
+                back_copy(k, q).start()
+        own_rows(q).start()
+
+    def own_rows(q):
+        return pltpu.make_async_copy(back_out.at[q, me], back_in.at[q, me], out_sem.at[q])
 
     activate(0)
-    pltpu.make_async_copy(wd, wd, load_sem.at[3]).wait()
+    pltpu.make_async_copy(wd, wd, load_sem.at[2]).wait()
     project(0, 0, FAR, DOWN, UP)
     take_piece(far, 1, 1)
     take_piece(down, 1, 1)
@@ -462,7 +507,6 @@
     send_joined(2, 0)
     send_free(1, 1)
     project(2, 1, UP, DOWN)
-    send_far(2, 1)
     send_free(2, 1)
     project(2, 1, HERE)
 
@@ -477,21 +521,23 @@
 
     collect(0, 0)
     send_joined(0, 1)
+    send_far(2, 1)
     collect(1, 0)
     send_joined(1, 1)
+    collect(0, 1)
     send_joined(2, 1)
     collect(2, 0)
-    collect(0, 1)
     collect(1, 1)
     collect(2, 1)
+    unpack_first(0)
     unpack(0)
+    unpack_first(1)
+    unpack_first(2)
     unpack(1)
+    unpack(2)
     relay_route.wait_recv()
     relay_x = remote(x_mid, x_in, relay_s.at[3], relay_r.at[2], to_across)
     relay_x.wait_recv()
-    unpack(2)
-    finish(0)
-    finish(1)
     for q in range(2):
         gather_sent(q)
     for src, dst, sem in (
@@ -502,11 +548,44 @@
     relay_first = remote(x_v, x_mid, relay_s.at[2], mid_r.at[0], to_across)
     for cp in (relay_route, relay_counts, relay_first, relay_x):
         cp.wait_send()
-    for q in range(strips - 1):
+    for q in range(strips):
+        own_rows(q).wait()
+        all_back_copies(q).wait_recv()
         all_back_copies(q).wait_send()
-    finish(2)
-    all_back_copies(2).wait_send()
-    pltpu.make_async_copy(out, out_hbm, out_sem.at[0]).wait()
+
+
+def finish(x_hbm, back_hbm, route_hbm, out_hbm, x_v, back_v, route_v, out_v, in_sem, out_sem):
+    strips, owners, cap, lanes = back_v.shape
+    part = strips * lanes
+    width = x_v.shape[1] // FINISH_STEPS
+    count = owners // FINISH_STEPS
+    load_route = pltpu.make_async_copy(route_hbm, route_v, in_sem.at[0])
+    load_route.start()
+    loads, stores = [], []
+    for i in range(FINISH_STEPS):
+        at, ks = pl.ds(i * width, width), pl.ds(i * count, count)
+        pair = (
+            pltpu.make_async_copy(back_hbm.at[:, ks], back_v.at[:, ks], in_sem.at[1 + 2 * i]),
+            pltpu.make_async_copy(x_hbm.at[:, at], x_v.at[:, at], in_sem.at[2 + 2 * i]),
+        )
+        for cp in pair:
+            cp.start()
+        loads.append(pair)
+        stores.append(pltpu.make_async_copy(out_v.at[:, at], out_hbm.at[:, at], out_sem.at[i]))
+    load_route.wait()
+    spread = route_v[:, :cap].astype(BF16)
+    weight = route_v[:, cap:cap + 1]
+    for i in range(FINISH_STEPS):
+        for cp in loads[i]:
+            cp.wait()
+        for k in range(i * count, (i + 1) * count):
+            rows = jnp.concatenate([back_v[q, k] for q in range(strips)], axis=1)
+            term = weight * jnp.dot(spread, rows, preferred_element_type=F32)
+            at = slice(k * part, (k + 1) * part)
+            out_v[:, at] = (x_v[:, at].astype(F32) + term).astype(BF16)
+        stores[i].start()
+    for cp in stores:
+        cp.wait()
 
 
 def solution(mesh):
@@ -523,20 +602,21 @@
         vmem = pltpu.VMEM
         dma = pltpu.SemaphoreType.DMA
         any_space = pl.BlockSpec(memory_space=pl.ANY)
-        return pl.pallas_call(
+        x_in, back, route = pl.pallas_call(
             functools.partial(kernel, sections),
-            out_shape=jax.ShapeDtypeStruct((tokens, width), BF16),
+            out_shape=(
+                jax.ShapeDtypeStruct((tokens, width), BF16),
+                jax.ShapeDtypeStruct((strips, MEMBERS, cap, LANES), BF16),
+                jax.ShapeDtypeStruct((tokens, tokens), F32),
+            ),
             in_specs=[any_space] * 7,
-            out_specs=any_space,
+            out_specs=(any_space,) * 3,
             scratch_shapes=[
-                vmem((tokens, width), BF16),
-                vmem((tokens, width), BF16),
                 vmem((tokens, width), BF16),
                 vmem((tokens, width), BF16),
                 vmem((1, width), F32),
                 vmem((2, tokens), jnp.int32),
                 vmem((2, tokens), F32),
-                vmem((tokens, tokens), F32),
                 vmem((tokens, tokens), F32),
                 vmem((MEMBERS, TILE, LANES), BF16),
                 vmem((MEMBERS, TILE, LANES), BF16),
@@ -563,15 +643,15 @@
                 vmem((strips, 2, 2, 2, half, LANES), BF16),
                 vmem((strips, 2, 2, half, LANES), BF16),
                 vmem((strips, 2, 2, half, LANES), BF16),
+                vmem((2, 2, CHIPS * cap, LANES), F32),
                 vmem((strips, MEMBERS, cap, LANES), BF16),
-                vmem((strips, MEMBERS, cap, LANES), BF16),
-                dma((7,)), dma((1,)),
+                dma((6 + X_LOADS,)), dma((strips,)),
                 dma((2,)), dma((2,)),
                 dma((2,)), dma((2, CHIPS, 2)), dma((2, CHIPS, 2)),
                 dma((1,)), dma((strips, 2, 4)),
                 dma((1,)), dma((strips, 2)),
+                dma((1,)), dma((strips, 2, 2)),
                 dma((1,)), dma((strips, 2)),
-                dma((1,)), dma((strips,)),
                 dma((strips,)), dma((strips,)),
                 dma((4,)), dma((3,)), dma((RELAY_PIECES,)),
             ],
@@ -588,6 +668,23 @@
             expert_ids.T,
             gate_weights.T,
         )
+        in_hbm = pl.BlockSpec(memory_space=pltpu.HBM)
+        return pl.pallas_call(
+            finish,
+            out_shape=jax.ShapeDtypeStruct((tokens, width), BF16),
+            in_specs=[in_hbm] * 3,
+            out_specs=in_hbm,
+            scratch_shapes=[
+                vmem((tokens, width), BF16),
+                vmem((strips, MEMBERS, cap, LANES), BF16),
+                vmem((tokens, tokens), F32),
+                vmem((tokens, width), BF16),
+                dma((1 + 2 * FINISH_STEPS,)),
+                dma((FINISH_STEPS,)),
+            ],
+            compiler_params=pltpu.CompilerParams(vmem_limit_bytes=62 * 2**20),
+            name="add_rows",
+        )(x_in, back, route)
 
     return jax.shard_map(
         per_device,

time: 91.4 us -> 88.1 us (0.964)
  local copies, waits for them, and re-layouts: 2.69 us -> 0 us
    unnamed x1 -> x0, local copies, waits for them, and re-layouts: 2.69 us -> none
    pallas_call x1 -> x2, Pallas kernels: 88.5 us -> 87.8 us  [the longest x1 84.8 us: per_device(): pl.pallas_call(functools.partial(kernel, sections), out_shape=(jax.ShapeD...]
where the time goes in v5:
time: 88.1 us; the launch traced here: 88 us
  Pallas kernels  87.8 us (100%)
    pallas_call x1, Pallas kernels, per_device(): pl.pallas_call(functools.partial(kernel, sections), out_shape=(jax.ShapeD...  84.8 us
    pallas_call x1, Pallas kernels, per_device(): pl.pallas_call(finish, out_shape=jax.ShapeDtypeStruct((tokens, width), BF...  2.98 us

profile of v5, /device:TPU:1, one launch (start us, length us, event | category | flops | bytes accessed | tf_op | source)
XLA Modules:
  0.0 88.0 jit_solution(7657524995394082444)
XLA Ops:
  0.0 84.8 %routed_block.1 = (bf16[128,6144]{1,0:T(8,128)(2,1)}, bf16[3,16,64,128]{3,2,1,0:T(8,128)(2,1)}, f32[128,128]{1,0:T(8,128)}) custom-call(bf16[128,6144]{1,0:T(8,128)(2,1)} %x_hbm.1, f32[1,6144]{1,0:T(1,128)} %gain_hbm.1, bf16[8,2,384,512]{3,2,1,0:T(8,128)(2,1)} %bitcast.5, bf16[8,2,384,512]{3,2,1,0:T(8,128)(2,1)} %bitcast.6, bf16[512,6144]{1,0:T(8,128)(2,1)} %bitcast.7, ...), custom_call_target="tpu_custom_call" | custom-call | tf_op jit(solution)/shard_map/routed_block/pallas_call | solution.py:605
  84.8 3.0 %add_rows.1 = bf16[128,6144]{1,0:T(8,128)(2,1)} custom-call(bf16[128,6144]{1,0:T(8,128)(2,1)} %get-tuple-element.8.x_hbm, bf16[3,16,64,128]{3,2,1,0:T(8,128)(2,1)} %get-tuple-element.9.back_hbm, f32[128,128]{1,0:T(8,128)} %get-tuple-element.10.route_hbm), custom_call_target="tpu_custom_call" | custom-call | tf_op jit(solution)/shard_map/add_rows/pallas_call | solution.py:672

commit v6 on v5

--- a/solution.py
+++ b/solution.py
@@ -142,13 +142,17 @@
         start, size = cuts[q]
         for t in range(4):
             i = j * 4 + t
-            at = pl.ds(pl.multiple_of(i * part + start, LANES), size)
+            offset = i * part + start
+            if not isinstance(j, int):
+                offset = pl.multiple_of(offset, LANES)
+            at = pl.ds(offset, size)
             n = (x_v[:, at].astype(F32) * scale * gain[:, at]).astype(BF16)
             packed[q][i, :cap] = jnp.dot(
                 spot_t, n, preferred_element_type=F32
             ).astype(BF16)
 
-    loop(0, MEMBERS // 4, lambda j: pack(j, 0))
+    for j in range(MEMBERS // 4):
+        pack(j, 0)
     pl.semaphore_wait(barrier, MEMBERS + 1)
 
     def slot_copy(k, q):
@@ -288,7 +292,6 @@
     multiply(up, 1, 0)
     multiply(far, 0, 0)
 
-    relay_on(1)
     take_piece(aup, 0, 0)
     take_piece(adown, 0, 1, to_up)
     send_piece(d, 1, 1, to_up)
@@ -303,13 +306,13 @@
     multiply(adown, 1, 0)
     multiply(far, 0, 1)
     multiply(aup, 0, 1)
+    relay_on(1)
     take_piece(far, 0, 1)
     take_piece(aup, 0, 1)
     take_piece(afar, 0, 0)
     multiply(far, 1, 0)
     multiply(aup, 1, 0)
     take_piece(aup, 1, 1, to_down)
-    relay_on(2)
     multiply(afar, 0, 0)
     take_piece(afar, 0, 1)
     multiply(aup, 1, 1)
@@ -473,6 +476,7 @@
     send_far(0, 0)
     send_free(0, 0)
     project(0, 0, HERE)
+    relay_on(2)
     project(1, 0, FAR, DOWN, UP)
     take_piece(afar, 1, 0)
     take_piece(adown, 1, 0)
@@ -484,12 +488,12 @@
     multiply(adown, 0, 1)
     project(1, 0, HERE)
     project(2, 0, FAR, DOWN, UP)
-    relay_on(3)
     take_piece(afar, 1, 1)
     take_piece(adown, 1, 1)
     send_far(2, 0)
     send_free(2, 0)
     project(2, 0, HERE)
+    relay_on(3)
     multiply(afar, 1, 1)
     multiply(adown, 1, 1)
     activate(1)

time: 88.1 us -> 87.6 us (level)
  no operation moved by 1% of the time
where the time goes in v6:
time: 87.6 us; the launch traced here: 87.5 us
  Pallas kernels  87.3 us (100%)
    pallas_call x1, Pallas kernels, per_device(): pl.pallas_call(functools.partial(kernel, sections), out_shape=(jax.ShapeD...  84.3 us
    pallas_call x1, Pallas kernels, per_device(): pl.pallas_call(finish, out_shape=jax.ShapeDtypeStruct((tokens, width), BF...  2.99 us

profile of v6, /device:TPU:1, one launch (start us, length us, event | category | flops | bytes accessed | tf_op | source)
XLA Modules:
  0.0 87.5 jit_solution(14491899545179490002)
XLA Ops:
  0.0 84.3 %routed_block.1 = (bf16[128,6144]{1,0:T(8,128)(2,1)}, bf16[3,16,64,128]{3,2,1,0:T(8,128)(2,1)}, f32[128,128]{1,0:T(8,128)}) custom-call(bf16[128,6144]{1,0:T(8,128)(2,1)} %x_hbm.1, f32[1,6144]{1,0:T(1,128)} %gain_hbm.1, bf16[8,2,384,512]{3,2,1,0:T(8,128)(2,1)} %bitcast.5, bf16[8,2,384,512]{3,2,1,0:T(8,128)(2,1)} %bitcast.6, bf16[512,6144]{1,0:T(8,128)(2,1)} %bitcast.7, ...), custom_call_target="tpu_custom_call" | custom-call | tf_op jit(solution)/shard_map/routed_block/pallas_call | solution.py:609
  84.3 3.0 %add_rows.1 = bf16[128,6144]{1,0:T(8,128)(2,1)} custom-call(bf16[128,6144]{1,0:T(8,128)(2,1)} %get-tuple-element.8.x_hbm, bf16[3,16,64,128]{3,2,1,0:T(8,128)(2,1)} %get-tuple-element.9.back_hbm, f32[128,128]{1,0:T(8,128)} %get-tuple-element.10.route_hbm), custom_call_target="tpu_custom_call" | custom-call | tf_op jit(solution)/shard_map/add_rows/pallas_call | solution.py:676

commit v7 on v6

--- a/solution.py
+++ b/solution.py
@@ -15,7 +15,7 @@
 LANES = 128
 RELAY_PIECES = 4
 X_LOADS = 4
-FINISH_STEPS = 4
+FINISH_STEPS = 2
 TILE = 16
 
 
@@ -97,9 +97,10 @@
     def greet(device):
         pl.semaphore_signal(barrier, inc=1, device_id=device, device_id_type=MESH)
 
-    loop(1, MEMBERS, lambda k: greet(member(k)[1]))
     greet((before, c, d))
     greet((before, c, across))
+    for k in range(MEMBERS - 1, 0, -1):
+        greet(member(k)[1])
 
     small[0].wait()
     small[1].wait()

time: 87.6 us -> 87.4 us (level)
  no operation moved by 1% of the time
where the time goes in v7:
time: 87.4 us; the launch traced here: 87.3 us
  Pallas kernels  87.1 us (100%)
    pallas_call x1, Pallas kernels, per_device(): pl.pallas_call(functools.partial(kernel, sections), out_shape=(jax.ShapeD...  84.2 us
    pallas_call x1, Pallas kernels, per_device(): pl.pallas_call(finish, out_shape=jax.ShapeDtypeStruct((tokens, width), BF...  2.93 us

profile of v7, /device:TPU:1, one launch (start us, length us, event | category | flops | bytes accessed | tf_op | source)
XLA Modules:
  0.0 87.3 jit_solution(6934009018378594486)
XLA Ops:
  0.0 84.2 %routed_block.1 = (bf16[128,6144]{1,0:T(8,128)(2,1)}, bf16[3,16,64,128]{3,2,1,0:T(8,128)(2,1)}, f32[128,128]{1,0:T(8,128)}) custom-call(bf16[128,6144]{1,0:T(8,128)(2,1)} %x_hbm.1, f32[1,6144]{1,0:T(1,128)} %gain_hbm.1, bf16[8,2,384,512]{3,2,1,0:T(8,128)(2,1)} %bitcast.5, bf16[8,2,384,512]{3,2,1,0:T(8,128)(2,1)} %bitcast.6, bf16[512,6144]{1,0:T(8,128)(2,1)} %bitcast.7, ...), custom_call_target="tpu_custom_call" | custom-call | tf_op jit(solution)/shard_map/routed_block/pallas_call | solution.py:610
  84.2 2.9 %add_rows.1 = bf16[128,6144]{1,0:T(8,128)(2,1)} custom-call(bf16[128,6144]{1,0:T(8,128)(2,1)} %get-tuple-element.8.x_hbm, bf16[3,16,64,128]{3,2,1,0:T(8,128)(2,1)} %get-tuple-element.9.back_hbm, f32[128,128]{1,0:T(8,128)} %get-tuple-element.10.route_hbm), custom_call_target="tpu_custom_call" | custom-call | tf_op jit(solution)/shard_map/add_rows/pallas_call | solution.py:677
